TPU v7x, 128 devices: a whole 4x4x4 slice. The times are simulated.
128 devices in a mesh: gx: 8 (over z, y_lo), gy: 16 (over y_hi, x, core).
Axes of the slice: x: 4, y: 4 (y_hi: 2, y_lo: 2; y = y_hi * 2 + y_lo), z: 4, core: 2. Of those that a mesh axis runs over, the one named last changes fastest.
Arguments:
- layer_input: bfloat16 [128, 128, 20, 1024], P('gx', 'gy'), may hold values from -6 to 6
- cotangent: bfloat16 [128, 128, 20, 1024], P('gx', 'gy'), may hold values from -6 to 6
- spectral_weight: bfloat16 [32, 32, 20, 20, 2, 256], P('gx', 'gy'), may hold values from -1.1953125 to 1.1953125
- mixer_weight: bfloat16 [20, 20], replicated, may hold values from -1.25 to 1.25
- bias_vector: float32 [20], replicated, may hold values from -3 to 3
Outputs:
- input_grad: bfloat16 [128, 128, 20, 1024], P('gx', 'gy')
- spectral_grad: float32 [32, 32, 20, 20, 2, 256], P('gx', 'gy')
- mixer_grad: float32 [20, 20], replicated
- bias_grad: float32 [20], replicated
All inputs are finite; a program needn't handle non-finite values.
Results may differ from a plain program's by a relative error of at most 0.038.
Values may be sent and summed in bfloat16 or wider, within the bound.
A program may use at most 192 MiB of HBM per device.

v0:
```python
import math

import jax
import jax.numpy as jnp
from jax import lax
from jax.sharding import PartitionSpec as P

NX = 128
NY = 128
NZ = 64
NT = 16
MZ = 16
MT = 8
KX = 32
KY = 32
KZT = 256
NZT = 1024


def signed_frequency(number):
    values = jnp.arange(number, dtype=jnp.int32)
    return jnp.where(values < number // 2, values, values - number)


def pair_table(frequency, length):
    places = jnp.arange(length, dtype=jnp.int32)
    phases = jnp.mod(frequency[:, None] * places[None, :], length).astype(jnp.float32)
    angles = phases * (-2.0 * math.pi / length)
    factor = float(length) ** (-0.5)
    cosine = jnp.cos(angles) * factor
    sine_part = jnp.sin(angles) * factor
    top_rows = jnp.stack([cosine, -sine_part], -1)
    low_rows = jnp.stack([sine_part, cosine], -1)
    return jnp.stack([top_rows, low_rows], 1).astype(jnp.bfloat16)


def depth_table():
    depth_freq = signed_frequency(2 * MZ)
    time_freq = jnp.arange(MT, dtype=jnp.int32)
    depth_pos = jnp.arange(NZ, dtype=jnp.int32)
    time_pos = jnp.arange(NT, dtype=jnp.int32)
    cell_count = NZ * NT
    phases = (
        depth_pos[:, None, None, None] * depth_freq[None, None, :, None] * NT
        + time_pos[None, :, None, None] * time_freq[None, None, None, :] * NZ
    )
    phases = jnp.mod(phases, cell_count).astype(jnp.float32).reshape(cell_count, 2 * MZ * MT)
    angles = phases * (-2.0 * math.pi / cell_count)
    factor = float(cell_count) ** (-0.5)
    stacked = jnp.stack([jnp.cos(angles) * factor, jnp.sin(angles) * factor], 1)
    return stacked.reshape(cell_count, 4 * MZ * MT).astype(jnp.bfloat16)


def mode_weight():
    orders = jnp.arange(2 * MZ * MT, dtype=jnp.int32) % MT
    return jnp.where(orders == 0, 1.0, 2.0).astype(jnp.float32)


def gelu_slope(values):
    normal_cdf = 0.5 * (1.0 + jax.scipy.special.erf(values * (1.0 / math.sqrt(2.0))))
    density = jnp.exp(-0.5 * values * values) * (1.0 / math.sqrt(2.0 * math.pi))
    return normal_cdf + values * density


def body(layer_input, cotangent, spectral_weight, mixer_weight, bias_vector):
    x_local = layer_input.shape[0]
    y_local = layer_input.shape[1]
    channels = layer_input.shape[2]
    x_table = pair_table(signed_frequency(KX), NX)
    y_table = pair_table(signed_frequency(KY), NY)
    depth_matrix = depth_table()
    weights_mode = mode_weight()
    x_rows = lax.dynamic_slice_in_dim(x_table, lax.axis_index("gx") * x_local, x_local, 2)
    y_rows = lax.dynamic_slice_in_dim(y_table, lax.axis_index("gy") * y_local, y_local, 2)

    def spectral_forward(grid):
        flattened = grid.reshape(-1, grid.shape[-1])
        depth_modes = jnp.dot(flattened, depth_matrix, preferred_element_type=jnp.float32)
        depth_modes = depth_modes.astype(jnp.bfloat16).reshape(x_local, y_local, channels, 2, KZT)
        window = y_rows
        y_modes = lax.psum_scatter(
            jnp.einsum(
                "lpyq,xycqk->lxcpk", window, depth_modes, preferred_element_type=jnp.float32
            ).astype(jnp.bfloat16),
            "gy",
            scatter_dimension=0,
            tiled=True,
        )
        window = x_rows
        return lax.psum_scatter(
            jnp.einsum(
                "apxq,lxcqk->alcpk", window, y_modes, preferred_element_type=jnp.float32
            ).astype(jnp.bfloat16),
            "gx",
            scatter_dimension=0,
            tiled=True,
        )

    def spectral_inverse(spectrum):
        window = x_rows
        inverse_x = jnp.einsum(
            "aqxp,alcqk->xlcpk",
            window,
            lax.all_gather(spectrum, "gx", axis=0, tiled=True),
            preferred_element_type=jnp.float32,
        ).astype(jnp.bfloat16)
        window = y_rows
        return jnp.einsum(
            "lqyp,xlcqk->xycpk",
            window,
            lax.all_gather(inverse_x, "gy", axis=1, tiled=True),
            preferred_element_type=jnp.float32,
        ).astype(jnp.bfloat16)

    def spatial_branch(spectrum):
        grid_modes = spectral_inverse(spectrum)
        flattened = grid_modes.reshape(-1, 2 * KZT)
        result = jnp.dot(flattened, depth_matrix.T, preferred_element_type=jnp.float32)
        return result.reshape(x_local, y_local, channels, -1)

    def contract(weights, values):
        return jnp.einsum("abiok,abik->abok", weights, values, preferred_element_type=jnp.float32)

    def adjoint(weights, values):
        return jnp.einsum("abiok,abok->abik", weights, values, preferred_element_type=jnp.float32)

    spectral_modes = spectral_forward(layer_input)
    weight_real = spectral_weight[:, :, :, :, 0]
    weight_imag = spectral_weight[:, :, :, :, 1]
    mode_real = spectral_modes[:, :, :, 0]
    mode_imag = spectral_modes[:, :, :, 1]
    real_sum = contract(weight_real, mode_real) - contract(weight_imag, mode_imag)
    imag_sum = contract(weight_real, mode_imag) + contract(weight_imag, mode_real)
    spectrum = (jnp.stack([real_sum, imag_sum], 3) * weights_mode).astype(jnp.bfloat16)
    branch = spatial_branch(spectrum)
    pointwise = jnp.einsum(
        "xyik,io->xyok", layer_input, mixer_weight, preferred_element_type=jnp.float32
    )
    pre_act = branch + pointwise + bias_vector[None, None, :, None]
    pre_grad = (cotangent * gelu_slope(pre_act)).astype(jnp.bfloat16)
    grad_modes = spectral_forward(pre_grad)
    scaled = grad_modes * weights_mode.astype(jnp.bfloat16)
    scaled_real = scaled[:, :, :, 0]
    scaled_imag = scaled[:, :, :, 1]
    back_real = adjoint(weight_real, scaled_real) + adjoint(weight_imag, scaled_imag)
    back_imag = adjoint(weight_real, scaled_imag) - adjoint(weight_imag, scaled_real)
    grad_spectrum = jnp.stack([back_real, back_imag], 3).astype(jnp.bfloat16)
    real_modes = mode_real.astype(jnp.float32)
    imag_modes = mode_imag.astype(jnp.float32)
    real_scaled = scaled_real.astype(jnp.float32)
    imag_scaled = scaled_imag.astype(jnp.float32)
    grad_real = (
        real_modes[:, :, :, None] * real_scaled[:, :, None]
        + imag_modes[:, :, :, None] * imag_scaled[:, :, None]
    )
    grad_imag = (
        real_modes[:, :, :, None] * imag_scaled[:, :, None]
        - imag_modes[:, :, :, None] * real_scaled[:, :, None]
    )
    spectral_grad = jnp.stack([grad_real, grad_imag], 4)
    grad_branch = spatial_branch(grad_spectrum)
    pointwise_back = jnp.einsum(
        "xyok,io->xyik", pre_grad, mixer_weight, preferred_element_type=jnp.float32
    )
    input_grad = (grad_branch + pointwise_back).astype(jnp.bfloat16)
    mixer_local = jnp.einsum(
        "xyik,xyok->io", layer_input, pre_grad, preferred_element_type=jnp.float32
    )
    bias_local = jnp.sum(pre_grad, axis=(0, 1, 3), dtype=jnp.float32)
    mixer_total, bias_total = lax.psum((mixer_local, bias_local), ("gx", "gy"))
    scale_factor = 1.0 / math.sqrt(NX * NY * NZT)
    return (input_grad, spectral_grad, mixer_total * scale_factor, bias_total * scale_factor)


def solution(mesh):
    return jax.shard_map(
        body,
        mesh=mesh,
        in_specs=(
            P("gx", "gy", None, None),
            P("gx", "gy", None, None),
            P("gx", "gy", None, None, None, None),
            P(),
            P(),
        ),
        out_specs=(P("gx", "gy", None, None), P("gx", "gy", None, None, None, None), P(), P()),
        check_vma=False,
    )
```

profile of v0, /device:TPU:1, one launch (start us, length us, event | category | flops | bytes accessed | tf_op | source)
XLA Modules:
  0.0 913.3 jit_solution(3742140586586021708)
XLA Ops:
  7.5 3.9 broadcast_add_fusion
  11.4 7.9 add.175
  19.6 4.3 multiply_convert_fusion.1
  23.9 0.8 copy-done.4
  25.0 1.3 copy.109
  26.4 8.8 copy.110
  35.2 9.0 reshape.355
  44.2 5.7 fusion.14
  49.9 2.6 copy.111
  52.5 3.5 reshape.356
  56.2 5.7 fusion.8
  61.9 14.0 %copy.114 = bf16[32,16,20,2,256]{4,1,3,2,0:T(8,128)(2,1)} copy(bf16[32,16,20,2,256]{4,0,3,2,1:T(8,128)(2,1)} %fusion.8) | data formatting | bytes 20971520 | tf_op jit(solution)/shard_map/convert_element_type | solution.py:84
  76.0 114.5 %reduce-scatter.5.cloned.1.call-done = bf16[2,16,20,2,256]{4,1,3,2,0:T(8,128)(2,1)} async-done(((bf16[32,16,20,2,256]{4,1,3,2,0:T(8,128)(2,1)}), bf16[2,16,20,2,256]{4,1,3,2,0:T(8,128)(2,1)}) %reduce-scatter.5.cloned.1.call-update) | async-done | bytes 655376 | tf_op jit(solution)/shard_map/reduce_scatter | solution.py:81
  190.5 2.7 fusion.35
  194.9 8.9 fusion.83
  203.8 68.4 %all-reduce.6.cloned.1.call-done = bf16[32,2,20,2,256]{4,0,3,2,1:T(8,128)(2,1)} async-done(((bf16[32,2,20,2,256]{4,0,3,2,1:T(8,128)(2,1)}), bf16[32,2,20,2,256]{4,0,3,2,1:T(8,128)(2,1)}) %all-reduce.6.cloned.1.call-update) | async-done | bytes 1310736
  272.2 1.8 bitcast_convert_fusion.13
  274.3 14.4 %fusion.17 = (f32[4,2,256,20]{2,1,3,0:T(2,128)S(1)}, f32[4,2,256,20]{2,1,3,0:T(2,128)S(1)}, f32[4,2,256,20]{2,1,3,0:T(2,128)S(1)}, f32[4,2,256,20]{2,1,3,0:T(2,1...) fusion(f32[4,2,256,20]{2,1,3,0:T(2,128)S(1)} %copy.269, ...), kind=kLoop, calls=%fused_computation.37 | loop fusion | flops 8028160 | bytes 7536640
  289.0 0.8 copy.118
  289.9 40.5 %all-gather.5.cloned.1.call-done = bf16[32,2,20,2,256]{4,3,2,1,0:T(2,128)(2,1)} async-done(((bf16[4,2,20,2,256]{4,3,2,1,0:T(2,128)(2,1)}), bf16[32,2,20,2,256]{4,3,2,1,0:T(2,128)(2,1)}) %all-gather.5.cloned.1.call-update) | async-done | bytes 1310736 | tf_op jit(solution)/shard_map/all_gather | solution.py:104
  330.4 2.7 fusion.44
  333.4 85.4 %all-gather.7.cloned.1.call-done = bf16[16,32,20,2,256]{4,0,3,2,1:T(8,128)(2,1)} async-done(((bf16[16,2,20,2,256]{4,0,3,2,1:T(8,128)(2,1)}), bf16[16,32,20,2,256]{4,0,3,2,1:T(8,128)(2,1)}) %all-gather.7.cloned.1.call-update) | async-done | bytes 10485776 | tf_op jit(solution)/shard_map/all_gather | solution.py:111
  418.9 22.4 %fusion.27 = bf16[16,8,20,2,256]{4,1,3,2,0:T(8,128)(2,1)S(1)} fusion(bf16[16,32,20,2,256,1]{4,0,3,2,1,5:T(8,128)(2,1)} %bitcast.256, bf16[32,2,8,2]{0,2,3,1:T(8,128)(2,1)S(1)} %copy.266), kind=kOutput, calls=%fused_computation.49 | convolution fusion | flops 169082880 | bytes 13109248 | tf_op jit(solution)/shard_map/lqyp,xlcqk->xycpk/dot_general | solution.py:108
  441.3 3.6 fusion.25
  445.0 16.6 %convert_reduce_fusion = (f32[20]{0:T(128)S(1)}, bf16[16,8,20,1024]{3,2,1,0:T(8,128)(2,1)}) fusion(f32[20]{0:T(128)S(1)} %copy-done.15, bf16[16,8,20,1024]{3,1,2,0:T(8,128)(2,1)S(1)} %bitcast.252, bf16[20,20]{1,0:T(8,128)(2,1)S(1)} %copy-done, f32[16,8,20,1024,1]{3,2,4,1,0:T(8,128)S(1)} %fusion.25, bf16[16,8,20,1024]{3,1,2,0:T(8,128)(2,1)S(1)} %bitcast.258), kind=kOutput, calls=%fused_computation.13 | convolution fusion | flops 144179184 | bytes 26215360 | tf_op jit(solution)/shard_map/xyik,io->xyok/dot_general | solution.py:136
  461.6 9.1 reshape.357
  470.7 6.7 convolution_convert_fusion
  477.4 3.5 reshape.358
  480.9 5.5 fusion.9
  486.4 14.0 %copy.127 = bf16[32,16,20,2,256]{4,1,3,2,0:T(8,128)(2,1)} copy(bf16[32,16,20,2,256]{4,0,3,2,1:T(8,128)(2,1)} %fusion.9) | data formatting | bytes 20971520 | tf_op jit(solution)/shard_map/convert_element_type | solution.py:84
  500.7 108.7 %reduce-scatter.7.cloned.1.call-done = bf16[2,16,20,2,256]{4,1,3,2,0:T(8,128)(2,1)} async-done(((bf16[32,16,20,2,256]{4,1,3,2,0:T(8,128)(2,1)}), bf16[2,16,20,2,256]{4,1,3,2,0:T(8,128)(2,1)}) %reduce-scatter.7.cloned.1.call-update) | async-done | bytes 655376 | tf_op jit(solution)/shard_map/reduce_scatter | solution.py:81
  609.3 2.7 fusion.36
  612.1 78.8 %all-reduce.8.cloned.1.call-done = bf16[32,2,20,2,256]{4,0,3,2,1:T(8,128)(2,1)} async-done(((bf16[32,2,20,2,256]{4,0,3,2,1:T(8,128)(2,1)}), bf16[32,2,20,2,256]{4,0,3,2,1:T(8,128)(2,1)}) %all-reduce.8.cloned.1.call-update) | async-done | bytes 1310736
  690.9 1.1 dynamic-slice_multiply_fusion
  692.0 0.8 bitcast_convert_fusion.9
  693.1 7.6 fusion.21
  701.2 0.8 copy.128
  702.0 40.6 %all-gather.9.cloned.1.call-done = bf16[32,2,20,2,256]{4,3,2,1,0:T(2,128)(2,1)} async-done(((bf16[4,2,20,2,256]{4,3,2,1,0:T(2,128)(2,1)}), bf16[32,2,20,2,256]{4,3,2,1,0:T(2,128)(2,1)}) %all-gather.9.cloned.1.call-update) | async-done | bytes 1310736 | tf_op jit(solution)/shard_map/all_gather | solution.py:104
  742.6 2.7 fusion.41
  745.4 0.7 copy.134
  746.1 11.5 %convolution_bitcast_fusion.2 = f32[20,20]{0,1:T(8,128)S(1)} fusion(bf16[16,8,20,1024]{3,2,1,0:T(8,128)(2,1)} %get-tuple-element.60, bf16[16,8,20,1024]{3,1,2,0:T(8,128)(2,1)} %param.5), kind=kOutput, calls=%fused_computation.68 | convolution fusion | flops 104857600 | bytes 10487360 | tf_op jit(solution)/shard_map/xyik,xyok->io/dot_general | solution.py:166
  757.6 82.4 %all-reduce.2 = (f32[20,20]{0,1:T(8,128)S(1)}, f32[20]{0:T(128)S(1)}) all-reduce(f32[20,20]{0,1:T(8,128)S(1)} %convolution_bitcast_fusion.2, f32[20]{0:T(128)S(1)} %get-tuple-element.59), channel_id=1, replica_groups=mesh['gx'=8,'gy'=16] {'gx','gy'}, use_global_device_ids=true, to_apply=%region_4.5 | all-reduce | flops 420 | bytes 3360 | tf_op jit(solution)/shard_map/psum | solution.py:170
  841.3 10.4 %multiply_add_fusion = (f32[4,2,20,20,1,256]{5,4,3,2,1,0:T(1,128)S(1)}, f32[4,2,20,20,1,256]{5,4,3,2,1,0:T(1,128)}) fusion(f32[4,2,20,256]{3,2,1,0:T(8,128)S(1)} %copy.137, f32[4,2,20,256]{3,2,1,0:T(8,128)S(1)} %copy.136, f32[4,2,20,256]{3,2,1,0:T(8,128)S(1)} %copy.135, f32[4,2,20,256]{3,2,1,0:T(8,128)} %copy.134), kind=kLoop, calls=%fused_computation.44 | loop fusion | flops 4915200 | bytes 7208960 | tf_op jit(solution)/shard_map/add | solution.py:153
  851.7 12.0 %pad_maximum_fusion = f32[4,2,20,20,2,256]{5,4,3,2,1,0:T(2,128)} fusion(f32[4,2,20,20,1,256]{5,4,3,2,1,0:T(1,128)} %get-tuple-element.49, f32[4,2,20,20,1,256]{5,4,3,2,1,0:T(1,128)S(1)} %get-tuple-element.48), kind=kLoop, calls=%fused_computation.20 | loop fusion | flops 1638400 | bytes 13107200 | tf_op jit(solution)/shard_map/stack | solution.py:160
  863.7 22.4 %fusion.28 = bf16[16,8,20,2,256]{4,1,3,2,0:T(8,128)(2,1)S(1)} fusion(bf16[16,32,20,2,256,1]{4,0,3,2,1,5:T(8,128)(2,1)} %bitcast.255, bf16[32,2,8,2]{0,2,3,1:T(8,128)(2,1)S(1)} %copy.266), kind=kOutput, calls=%fused_computation.50 | convolution fusion | flops 169082880 | bytes 13109248 | tf_op jit(solution)/shard_map/lqyp,xlcqk->xycpk/dot_general | solution.py:108
  886.1 6.7 fusion.23
  892.8 7.4 fusion.6
  900.2 5.8 copy.139
  (94 shorter events, 5.6 us)
Async XLA Ops:
  7.2 437.8 %copy-start = (bf16[20,20]{1,0:T(8,128)(2,1)S(1)}, bf16[20,20]{1,0:T(8,128)(2,1)}, u32[]{:S(2)}) copy-start(bf16[20,20]{1,0:T(8,128)(2,1)} %param.8) | copy-start | bytes 2404
  7.2 183.3 %reduce-scatter.5.cloned.1.call-start = ((), (), s32[]{:S(2)}) async-start(), calls=%async_computation.2 | async-start | bytes 11141120 | tf_op jit(solution)/shard_map/reduce_scatter | solution.py:81
  23.9 0.8 copy-start.4
  23.9 1.0 copy-start.7
  75.9 117.8 %copy-start.16 = (u32[128]{0:T(128)S(1)}, u32[128]{0:T(128)}, u32[]{:S(2)}) copy-start(u32[128]{0:T(128)} %constant.106) | copy-start | bytes 1540
  75.9 119.1 %copy-start.1 = (bf16[4,2,20,20,2,256]{5,4,3,2,1,0:T(2,128)(2,1)S(1)}, bf16[4,2,20,20,2,256]{5,4,3,2,1,0:T(2,128)(2,1)}, u32[]{:S(2)}) copy-start(bf16[4,2,20,20,2,256]{5,4,3,2,1,0:T(2,128)(2,1)} %param.7) | copy-start | bytes 9830404
  75.9 196.3 %all-reduce.6.cloned.1.call-start = ((), (), s32[]{:S(2)}) async-start(), calls=%async_computation.8 | async-start | bytes 2621440
  193.2 137.2 %all-gather.5.cloned.1.call-start = ((), (), s32[]{:S(2)}) async-start(), calls=%async_computation.3 | async-start | bytes 1474560 | tf_op jit(solution)/shard_map/all_gather | solution.py:104
  289.8 129.1 %all-gather.7.cloned.1.call-start = ((), (), s32[]{:S(2)}) async-start(), calls=%async_computation.4 | async-start | bytes 11141120 | tf_op jit(solution)/shard_map/all_gather | solution.py:111
  333.1 276.2 %reduce-scatter.7.cloned.1.call-start = ((), (), s32[]{:S(2)}) async-start(), calls=%async_computation.5 | async-start | bytes 11141120 | tf_op jit(solution)/shard_map/reduce_scatter | solution.py:81
  418.8 22.4 %copy-start.5 = (bf16[1024,1,256]{2,0,1:T(8,128)(2,1)S(1)}, bf16[1024,1,256]{2,0,1:T(8,128)(2,1)}, u32[]{:S(2)}) copy-start(bf16[1024,1,256]{2,0,1:T(8,128)(2,1)} %copy-done.4) | copy-start | bytes 1572868
  418.8 22.4 %copy-start.8 = (bf16[1024,1,256]{2,0,1:T(8,128)(2,1)S(1)}, bf16[1024,1,256]{2,0,1:T(8,128)(2,1)}, u32[]{:S(2)}) copy-start(bf16[1024,1,256]{2,0,1:T(8,128)(2,1)} %copy-done.7) | copy-start | bytes 1572868
  418.8 26.1 %slice-start.2 = ((s8[5242880]{0:T(1024)(128)(4,1)}), s8[1048576]{0:T(1024)(128)(4,1)S(1)}, s32[]{:S(2)}) async-start(s8[5242880]{0:T(1024)(128)(4,1)} %bitcast.251), calls=%async_computation.12 | async-start | bytes 2097152
  418.9 26.1 %slice-start.4 = ((s8[5242880]{0:T(1024)(128)(4,1)}), s8[4194304]{0:T(1024)(128)(4,1)S(1)}, s32[]{:S(2)}) async-start(s8[5242880]{0:T(1024)(128)(4,1)} %bitcast.257), calls=%async_computation.14 | async-start | bytes 8388608
  441.2 3.7 slice-start.3
  441.3 3.7 slice-start.5
  441.3 3.7 copy-start.15
  461.6 9.1 copy-start.10
  500.4 192.7 %copy-start.2 = (bf16[4,2,20,20,1,256]{5,1,3,2,0,4:T(2,128)(2,1)S(1)}, bf16[4,2,20,20,1,256]{5,1,3,2,0,4:T(2,128)(2,1)}, u32[]{:S(2)}) copy-start(bf16[4,2,20,20,1,256]{5,1,3,2,0,4:T(2,128)(2,1)} %get-tuple-element.38) | copy-start | bytes 4915204
  500.4 192.7 %copy-start.3 = (bf16[4,2,20,20,1,256]{5,1,3,2,0,4:T(2,128)(2,1)S(1)}, bf16[4,2,20,20,1,256]{5,1,3,2,0,4:T(2,128)(2,1)}, u32[]{:S(2)}) copy-start(bf16[4,2,20,20,1,256]{5,1,3,2,0,4:T(2,128)(2,1)} %get-tuple-element.39) | copy-start | bytes 4915204
  500.4 190.5 %all-reduce.8.cloned.1.call-start = ((), (), s32[]{:S(2)}) async-start(), calls=%async_computation.9 | async-start | bytes 2621440
  612.0 130.6 %all-gather.9.cloned.1.call-start = ((), (), s32[]{:S(2)}) async-start(), calls=%async_computation.6 | async-start | bytes 1474560 | tf_op jit(solution)/shard_map/all_gather | solution.py:104
  700.8 44.5 %copy-start.12 = (f32[4,2,20,256]{3,0,2,1:T(4,128)S(1)}, f32[4,2,20,256]{3,0,2,1:T(4,128)}, u32[]{:S(2)}) copy-start(f32[4,2,20,256]{3,0,2,1:T(4,128)} %get-tuple-element.45) | copy-start | bytes 491524
  700.8 44.6 %copy-start.11 = (f32[4,2,20,256]{3,0,2,1:T(4,128)S(1)}, f32[4,2,20,256]{3,0,2,1:T(4,128)}, u32[]{:S(2)}) copy-start(f32[4,2,20,256]{3,0,2,1:T(4,128)} %get-tuple-element.42) | copy-start | bytes 491524
  702.0 161.7 %all-gather.11.cloned.1.call-start = ((), (), s32[]{:S(2)}) async-start(), calls=%async_computation.7 | async-start | bytes 11141120 | tf_op jit(solution)/shard_map/all_gather | solution.py:111
  746.1 95.1 %copy-start.14 = (f32[4,2,20,256]{3,0,2,1:T(4,128)S(1)}, f32[4,2,20,256]{3,0,2,1:T(4,128)}, u32[]{:S(2)}) copy-start(f32[4,2,20,256]{3,0,2,1:T(4,128)} %get-tuple-element.53) | copy-start | bytes 491524
  746.1 95.1 %copy-start.13 = (f32[4,2,20,256]{3,0,2,1:T(4,128)S(1)}, f32[4,2,20,256]{3,0,2,1:T(4,128)}, u32[]{:S(2)}) copy-start(f32[4,2,20,256]{3,0,2,1:T(4,128)} %get-tuple-element.50) | copy-start | bytes 491524
  863.7 22.4 %copy-start.6 = (bf16[1024,1,256]{2,0,1:T(8,128)(2,1)S(1)}, bf16[1024,1,256]{2,0,1:T(8,128)(2,1)}, u32[]{:S(2)}) copy-start(bf16[1024,1,256]{2,0,1:T(8,128)(2,1)} %copy-done.4) | copy-start | bytes 1572868
  863.7 22.4 %copy-start.9 = (bf16[1024,1,256]{2,0,1:T(8,128)(2,1)S(1)}, bf16[1024,1,256]{2,0,1:T(8,128)(2,1)}, u32[]{:S(2)}) copy-start(bf16[1024,1,256]{2,0,1:T(8,128)(2,1)} %copy-done.7) | copy-start | bytes 1572868
  863.7 29.1 %slice-start = ((s8[6291456]{0:T(1024)(128)(4,1)}), s8[4194304]{0:T(1024)(128)(4,1)S(1)}, s32[]{:S(2)}) async-start(s8[6291456]{0:T(1024)(128)(4,1)} %bitcast.247), calls=%async_computation.10 | async-start | bytes 8388608
  886.1 6.7 slice-start.1
Sparse Core Ops, SparseCore 0:
  76.0 114.4 reduce-scatter.4
  193.3 78.8 all-reduce.5
  289.9 40.4 all-gather.4
  333.6 85.2 all-gather.6
  500.5 108.7 reduce-scatter.6
  612.3 78.6 all-reduce.7
  702.1 40.4 all-gather.8
  745.4 86.1 all-gather.10
where the time goes:
time: 923 us; the launch traced here: 913 us
  waiting for transfers between devices  537 us (58%)
  matrix products  125 us (14%)
  local copies, waits for them, and re-layouts  94.2 us (10%)
  blocking collectives  82.4 us (9%)
  other arithmetic  58 us (6%)
  between operations  15.8 us (2%)
    reduce_scatter x2, waiting for transfers between devices, spectral_forward(): lax.psum_scatter(jnp.einsum('lpyq,xycqk->lxcpk', window, depth_modes, pre...  223 us
    unnamed x10, waiting for transfers between devices  147 us
    all_gather x2, waiting for transfers between devices, spectral_inverse(): lax.all_gather(inverse_x, 'gy', axis=1, tiled=True)  85.4 us
    psum x1, blocking collectives, body(): mixer_total, bias_total = lax.psum((mixer_local, bias_local), ('gx', 'gy'))  82.4 us
    all_gather x2, waiting for transfers between devices, spectral_inverse(): lax.all_gather(spectrum, 'gx', axis=0, tiled=True)  81.1 us
    dot_general x2, matrix products, spectral_inverse(): jnp.einsum('lqyp,xlcqk->xycpk', window, lax.all_gather(inverse_x, 'gy', a...  44.7 us
    convert_element_type x2, local copies, waits for them, and re-layouts, spectral_forward(): y_modes = lax.psum_scatter(jnp.einsum('lpyq,xycqk->lxcpk', window, depth_...  27.9 us
    unnamed x5, other arithmetic  22 us
  transfers between devices with their start and end apart: 8, of which 7 were waited for; matrix products, arithmetic and copies ran while one was open for 5% of the time, Pallas kernels for 0%

commit v1 on v0

v1 whole, which is shorter than its diff:
```python
import functools
import math

import jax
import jax.numpy as jnp
import ml_dtypes
import numpy as np
from jax import lax
from jax.experimental import pallas as pl
from jax.experimental.pallas import tpu as pltpu
from jax.sharding import PartitionSpec as P

NX = 128
NY = 128
NZ = 64
NT = 16
C = 20
MZ = 16
MT = 8
KX = 32
KY = 32
KZT = 256
NZT = 1024
GX = 8
GY = 16
HALF = 8
XL = NX // GX
YL = NY // GY
CHUNKS = 5
CC = C // CHUNKS
ROWS = C * YL
CR = CC * YL
BF = jnp.bfloat16
F32 = jnp.float32
MESH = pl.DeviceIdType.MESH


def signed_frequency(number):
    values = np.arange(number)
    return np.where(values < number // 2, values, values - number)


def pair_table(frequency, length):
    places = np.arange(length)
    phases = np.mod(frequency[:, None] * places[None, :], length)
    angles = phases * (-2.0 * math.pi / length)
    factor = float(length) ** (-0.5)
    cosine = np.cos(angles) * factor
    sine_part = np.sin(angles) * factor
    top_rows = np.stack([cosine, -sine_part], -1)
    low_rows = np.stack([sine_part, cosine], -1)
    return np.stack([top_rows, low_rows], 1)


def depth_table():
    fz = signed_frequency(2 * MZ)
    ft = np.arange(MT)
    z = np.arange(NZ)
    t = np.arange(NT)
    phases = (
        z[:, None, None, None] * fz[None, None, :, None] * NT
        + t[None, :, None, None] * ft[None, None, None, :] * NZ
    )
    phases = np.mod(phases, NZT).reshape(NZT, KZT)
    angles = phases * (-2.0 * math.pi / NZT)
    factor = float(NZT) ** (-0.5)
    stacked = np.stack([np.cos(angles) * factor, np.sin(angles) * factor], 1)
    return stacked.reshape(NZT, 2 * KZT)


def as_bf16(table):
    return np.ascontiguousarray(table).astype(np.float32).astype(ml_dtypes.bfloat16)


@functools.lru_cache(maxsize=None)
def tables():
    depth = depth_table()
    xt = pair_table(signed_frequency(KX), NX)
    yt = pair_table(signed_frequency(KY), NY)
    eye_c = np.eye(CC)
    eye_l = np.eye(2)
    yv = yt.reshape(GY, 2, 2, 2, HALF, YL, 2)
    yf = np.einsum("jlphsyq,cd->hjcplsdqy", yv, eye_c).reshape(2, 256, 512)
    xv = xt.reshape(GX, 4, 2, GX, HALF, 2, 2)
    xf = np.einsum("iapgsxq,cd,lm->giacplsxdqm", xv, eye_c, eye_l).reshape(GX, 512, 256)
    xi = np.transpose(xf, (0, 2, 1))
    xf = np.concatenate([xf, xf], 2)
    yi = np.transpose(yf, (0, 2, 1))
    return tuple(as_bf16(v) for v in (depth, depth.T, yf, yi, xf, xi))


def mode_weight():
    orders = jnp.arange(KZT, dtype=jnp.int32) % MT
    return jnp.where(orders == 0, 1.0, 2.0).astype(F32)


def gelu_slope(values):
    normal_cdf = 0.5 * (1.0 + lax.erf(values * (1.0 / math.sqrt(2.0))))
    density = jnp.exp(-0.5 * values * values) * (1.0 / math.sqrt(2.0 * math.pi))
    return normal_cdf + values * density


def mm(a, b):
    return jnp.dot(a, b, preferred_element_type=F32)


class Place:
    def __init__(self):
        self.gx = lax.axis_index("gx")
        self.gy = lax.axis_index("gy")
        self.lo = lax.rem(self.gy, HALF)
        self.hi = lax.div(self.gy, HALF)

    def x_peer(self, d):
        return lax.rem(self.gx + d, GX)

    def y_peer(self, d):
        return lax.rem(self.gy + d, GY)

    def half_peer(self, d):
        return lax.rem(self.lo + d, HALF)

    def greet(self):
        barrier = pltpu.get_barrier_semaphore()
        for d in range(1, GX):
            pl.semaphore_signal(
                barrier, inc=1, device_id={"gx": self.x_peer(d)}, device_id_type=MESH
            )
        for d in range(1, GY):
            pl.semaphore_signal(
                barrier, inc=1, device_id={"gy": self.y_peer(d)}, device_id_type=MESH
            )
        pl.semaphore_wait(barrier, GX + GY - 2)


def remote(src, dst, send, recv, device):
    pltpu.make_async_remote_copy(
        src_ref=src, dst_ref=dst, send_sem=send, recv_sem=recv,
        device_id=device, device_id_type=MESH,
    ).start()


def local(src, dst, sem):
    pltpu.make_async_copy(src, dst, sem).start()


def wait_for(region, sem):
    pltpu.make_async_copy(region, region, sem).wait()


def half_exchange(me, src, dst, send, recv):
    for d in range(1, HALF):
        peer = me.half_peer(d)
        remote(src.at[peer], dst.at[me.lo], send, recv, {"gy": me.hi * HALF + peer})
    local(src.at[me.lo], dst.at[me.lo], recv)


def row_exchange(me, src, dst, send, recv):
    for d in range(1, GY):
        peer = me.y_peer(d)
        remote(src.at[peer], dst.at[me.gy], send, recv, {"gy": peer})
    local(src.at[me.gy], dst.at[me.gy], recv)


def row_spread(me, src, dst, send, recv):
    for d in range(1, GY):
        peer = me.y_peer(d)
        remote(src.at[lax.rem(peer, HALF)], dst.at[me.gy], send, recv, {"gy": peer})
    local(src.at[me.lo], dst.at[me.gy], recv)


def column_exchange(me, src, dst, send, recv):
    for d in range(1, GX):
        peer = me.x_peer(d)
        remote(src.at[peer], dst.at[me.gx], send, recv, {"gx": peer})
    local(src.at[me.gx], dst.at[me.gx], recv)


def column_spread(me, src, dst, send, recv):
    for d in range(1, GX):
        remote(src, dst.at[me.gx], send, recv, {"gx": me.x_peer(d)})
    local(src, dst.at[me.gx], recv)


FORWARD_SCRATCH = [
    pltpu.VMEM((CHUNKS, HALF, 128, KZT), BF),
    pltpu.VMEM((CHUNKS, HALF, 128, KZT), BF),
    pltpu.VMEM((CHUNKS, GY, 32, KZT), BF),
    pltpu.VMEM((CHUNKS, GY, 32, KZT), BF),
    pltpu.VMEM((CHUNKS, GX, 64, KZT), BF),
    pltpu.VMEM((CHUNKS, GX, 64, KZT), BF),
    pltpu.SemaphoreType.DMA((3, CHUNKS)),
    pltpu.SemaphoreType.DMA((3, CHUNKS)),
]
INVERSE_SCRATCH = [
    pltpu.VMEM((CHUNKS, GX, 64, KZT), BF),
    pltpu.VMEM((CHUNKS, HALF, 32, KZT), BF),
    pltpu.VMEM((CHUNKS, GY, 32, KZT), BF),
    pltpu.VMEM((CHUNKS, HALF, 128, KZT), BF),
    pltpu.VMEM((CHUNKS, HALF, 128, KZT), BF),
    pltpu.SemaphoreType.DMA((3, CHUNKS)),
    pltpu.SemaphoreType.DMA((3, CHUNKS)),
]


class Forward:
    def __init__(self, me, depth, yf, xf, out, sa, ra, sb, rb, sc, rc, send, recv):
        self.me, self.depth, self.yf, self.xf, self.out = me, depth, yf, xf, out
        self.sa, self.ra, self.sb, self.rb, self.sc, self.rc = sa, ra, sb, rb, sc, rc
        self.send, self.recv = send, recv

    def put(self, c, part, parts, grid):
        count = XL // parts
        modes = mm(grid, self.depth[...])
        real = modes[:, :KZT].reshape(count, CC, 1, YL, KZT)
        imag = modes[:, KZT:].reshape(count, CC, 1, YL, KZT)
        both = jnp.concatenate([real, imag], 2).reshape(count * 64, KZT).astype(BF)
        self.sa[c, pl.ds(part * (count // 2), count // 2)] = both.reshape(count // 2, 128, KZT)

    def send_a(self, c):
        half_exchange(
            self.me, self.sa.at[c], self.ra.at[c], self.send.at[0, c], self.recv.at[0, c]
        )

    def stage_b(self, c):
        wait_for(self.ra.at[c], self.recv.at[0, c])
        for x2 in range(2):
            block = self.ra[c, :, x2 * 64 : x2 * 64 + 64, :].reshape(512, KZT)
            self.sb[c, :, x2 * 16 : x2 * 16 + 16, :] = (
                mm(self.yf[...], block).astype(BF).reshape(GY, 16, KZT)
            )
        row_exchange(
            self.me, self.sb.at[c], self.rb.at[c], self.send.at[1, c], self.recv.at[1, c]
        )

    def stage_c(self, c):
        wait_for(self.rb.at[c], self.recv.at[1, c])
        block = self.rb[c].reshape(512, KZT)
        self.sc[c] = mm(self.xf[...], block).astype(BF).reshape(GX, 64, KZT)
        column_exchange(
            self.me, self.sc.at[c], self.rc.at[c], self.send.at[2, c], self.recv.at[2, c]
        )

    def stage_d(self, c):
        wait_for(self.rc.at[c], self.recv.at[2, c])
        total = self.rc[c, 0].astype(F32)
        for source in range(1, GX):
            total = total + self.rc[c, source].astype(F32)
        self.out[c] = total.astype(BF)

    def finish(self):
        @pl.loop(0, CHUNKS)
        def _(c):
            wait_for(self.sa.at[c, pl.ds(0, HALF - 1)], self.send.at[0, c])
            wait_for(self.sb.at[c, pl.ds(0, GY - 1)], self.send.at[1, c])
            wait_for(self.sc.at[c, pl.ds(0, GX - 1)], self.send.at[2, c])


class Inverse:
    def __init__(self, me, back, yi, xi, spec, rp, sq, rq, sr, rr, send, recv):
        self.me, self.back, self.yi, self.xi, self.spec = me, back, yi, xi, spec
        self.rp, self.sq, self.rq, self.sr, self.rr = rp, sq, rq, sr, rr
        self.send, self.recv = send, recv

    def stage_p(self, c):
        column_spread(
            self.me, self.spec.at[c], self.rp.at[c], self.send.at[0, c], self.recv.at[0, c]
        )

    def stage_q(self, c):
        wait_for(self.rp.at[c], self.recv.at[0, c])
        block = self.rp[c].reshape(512, KZT)
        self.sq[c] = mm(self.xi[...], block).astype(BF).reshape(HALF, 32, KZT)
        row_spread(
            self.me, self.sq.at[c], self.rq.at[c], self.send.at[1, c], self.recv.at[1, c]
        )

    def stage_r(self, c):
        wait_for(self.rq.at[c], self.recv.at[1, c])
        for x2 in range(2):
            block = self.rq[c, :, x2 * 16 : x2 * 16 + 16, :].reshape(256, KZT)
            self.sr[c, :, x2 * 64 : x2 * 64 + 64, :] = (
                mm(self.yi[...], block).astype(BF).reshape(HALF, 64, KZT)
            )
        half_exchange(
            self.me, self.sr.at[c], self.rr.at[c], self.send.at[2, c], self.recv.at[2, c]
        )

    def ready(self, c):
        wait_for(self.rr.at[c], self.recv.at[2, c])

    def branch(self, c, part, parts):
        count = XL // parts
        block = self.rr[c, pl.ds(part * (count // 2), count // 2)].astype(F32)
        block = block.reshape(count, CC, 2, YL, KZT)
        real = block[:, :, 0].reshape(count * CR, KZT).astype(BF)
        imag = block[:, :, 1].reshape(count * CR, KZT).astype(BF)
        return mm(real, self.back[:KZT, :]) + mm(imag, self.back[KZT:, :])

    def finish(self):
        @pl.loop(0, CHUNKS)
        def _(c):
            wait_for(self.rp.at[c, pl.ds(0, GX - 1)], self.send.at[0, c])
            wait_for(self.rq.at[c, pl.ds(0, GY - 1)], self.send.at[1, c])
            wait_for(self.sr.at[c, pl.ds(0, HALF - 1)], self.send.at[2, c])


def staged(stages):
    depth = len(stages)

    @pl.loop(0, CHUNKS + depth - 1)
    def _(t):
        for s, stage in enumerate(stages):
            @pl.when(jnp.logical_and(t >= s, t < CHUNKS + s))
            def _(stage=stage, s=s):
                stage(t - s)


def first_kernel(x_hbm, depth, yf, xf, out, xbuf, xsem, *scratch):
    me = Place()

    @pl.loop(0, CHUNKS)
    def _(c):
        local(x_hbm.at[:, pl.ds(c * CR, CR), :], xbuf.at[c], xsem.at[c])

    me.greet()
    fwd = Forward(me, depth, yf, xf, out, *scratch)

    def stage_a(c):
        wait_for(xbuf.at[c], xsem.at[c])
        for part in range(2):
            fwd.put(c, part, 2, xbuf[c, part * 8 : part * 8 + 8].reshape(8 * CR, NZT))
        fwd.send_a(c)

    staged([stage_a, fwd.stage_b, fwd.stage_c, fwd.stage_d])
    fwd.finish()


def second_kernel(
    x_hbm, cot_hbm, spec, mixer, bias, depth, back, yf, yi, xf, xi, grad_hbm, out,
    xbuf, cbuf, gbuf, point, xsem, csem, gsem, *scratch
):
    me = Place()
    local(x_hbm, xbuf, xsem)

    @pl.loop(0, CHUNKS)
    def _(c):
        local(cot_hbm.at[:, pl.ds(c * CR, CR), :], cbuf.at[c], csem.at[c])

    me.greet()
    n_inverse = len(INVERSE_SCRATCH)
    inv = Inverse(me, back, yi, xi, spec, *scratch[:n_inverse])
    fwd = Forward(me, depth, yf, xf, out, *scratch[n_inverse:])

    @pl.loop(0, CHUNKS)
    def _(c):
        inv.stage_p(c)

    wait_for(xbuf, xsem)

    @pl.loop(0, XL)
    def _(x):
        point[x] = mm(mixer[...], xbuf[x]) + bias[...]

    def stage_s(c):
        inv.ready(c)
        wait_for(cbuf.at[c], csem.at[c])

        @pl.loop(0, 2)
        def _(part):
            rows = pl.ds(part * 8, 8)
            pre = inv.branch(c, part, 2)
            pre = pre + point[rows, pl.ds(c * CR, CR), :].reshape(8 * CR, NZT)
            cot = cbuf[c, rows].reshape(8 * CR, NZT).astype(F32)
            grad = (cot * gelu_slope(pre)).astype(BF)
            gbuf[c, rows] = grad.reshape(8, CR, NZT)
            fwd.put(c, part, 2, grad)

        local(gbuf.at[c], grad_hbm.at[:, pl.ds(c * CR, CR), :], gsem.at[c])
        fwd.send_a(c)

    staged([inv.stage_q, inv.stage_r, stage_s, fwd.stage_b, fwd.stage_c, fwd.stage_d])

    @pl.loop(0, CHUNKS)
    def _(c):
        wait_for(gbuf.at[c], gsem.at[c])

    inv.finish()
    fwd.finish()


def third_kernel(
    x_hbm, grad_hbm, spec, mixer, fold, back, yi, xi, out_hbm, small_out,
    xbuf, gbuf, obuf, point, mixed, one, col, two, row, xsem, gsem, osem, small, *scratch
):
    me = Place()
    local(x_hbm, xbuf, xsem)
    local(grad_hbm, gbuf, gsem)
    me.greet()
    inv = Inverse(me, back, yi, xi, spec, *scratch)

    @pl.loop(0, CHUNKS)
    def _(c):
        inv.stage_p(c)

    wait_for(xbuf, xsem)
    wait_for(gbuf, gsem)
    mixed[...] = jnp.zeros_like(mixed)

    @pl.loop(0, XL)
    def _(x):
        grad = gbuf[x]
        point[x] = mm(mixer[...], grad)
        contract = (((1,), (1,)), ((), ()))
        mixed[:ROWS, :] += lax.dot_general(xbuf[x], grad, contract, preferred_element_type=F32)
        mixed[ROWS:, :] += lax.dot_general(
            jnp.ones((8, NZT), BF), grad, contract, preferred_element_type=F32
        )

    places = mixed[:ROWS, :].shape
    same = lax.rem(lax.broadcasted_iota(jnp.int32, places, 0), YL) == lax.rem(
        lax.broadcasted_iota(jnp.int32, places, 1), YL
    )
    kept = jnp.where(same, mixed[:ROWS, :], 0.0).reshape(C, YL, ROWS).sum(1)
    stacked = jnp.concatenate([kept, mixed[ROWS : ROWS + 4, :]], 0)
    one[...] = lax.dot_general(
        stacked, fold[...], (((1,), (0,)), ((), ())),
        precision=lax.Precision.HIGHEST, preferred_element_type=F32,
    )
    for d in range(1, GX):
        remote(one, col.at[me.gx], small.at[0], small.at[1], {"gx": me.x_peer(d)})
    local(one, col.at[me.gx], small.at[1])

    def stage_s(c):
        inv.ready(c)

        @pl.loop(0, 2)
        def _(part):
            rows = pl.ds(part * 8, 8)
            total = inv.branch(c, part, 2)
            total = total + point[rows, pl.ds(c * CR, CR), :].reshape(8 * CR, NZT)
            obuf[c, rows] = total.astype(BF).reshape(8, CR, NZT)

        local(obuf.at[c], out_hbm.at[:, pl.ds(c * CR, CR), :], osem.at[c])

    staged([inv.stage_q, inv.stage_r, stage_s])

    wait_for(col, small.at[1])
    total = col[0]
    for source in range(1, GX):
        total = total + col[source]
    two[...] = total
    for d in range(1, GY):
        remote(two, row.at[me.gy], small.at[2], small.at[3], {"gy": me.y_peer(d)})
    local(two, row.at[me.gy], small.at[3])
    wait_for(row, small.at[3])
    total = row[0]
    for source in range(1, GY):
        total = total + row[source]
    small_out[...] = total
    wait_for(col.at[pl.ds(0, GX - 1)], small.at[0])
    wait_for(row.at[pl.ds(0, GY - 1)], small.at[2])

    @pl.loop(0, CHUNKS)
    def _(c):
        wait_for(obuf.at[c], osem.at[c])

    inv.finish()


ANY = pl.BlockSpec(memory_space=pl.ANY)
VM = pl.BlockSpec(memory_space=pltpu.VMEM)


def params(number):
    return pltpu.CompilerParams(
        collective_id=number, has_side_effects=True, vmem_limit_bytes=60 * 2**20
    )


def body(layer_input, cotangent, spectral_weight, mixer_weight, bias_vector):
    depth, back, yf_all, yi_all, xf_all, xi_all = (jnp.asarray(v) for v in tables())
    gx = lax.axis_index("gx")
    half = lax.axis_index("gy") // HALF
    yf = lax.dynamic_index_in_dim(yf_all, half, 0, False)
    yi = lax.dynamic_index_in_dim(yi_all, half, 0, False)
    xf = lax.dynamic_index_in_dim(xf_all, gx, 0, False)
    xi = lax.dynamic_index_in_dim(xi_all, gx, 0, False)
    weights_mode = mode_weight()
    grid = jnp.swapaxes(layer_input, 1, 2).reshape(XL, ROWS, NZT)
    cot = jnp.swapaxes(cotangent, 1, 2).reshape(XL, ROWS, NZT)
    eye = jnp.eye(YL, dtype=BF)
    mixer_forward = jnp.einsum("io,yz->oyiz", mixer_weight, eye).reshape(ROWS, ROWS)
    mixer_back = jnp.einsum("io,yz->iyoz", mixer_weight, eye).reshape(ROWS, ROWS)
    bias_rows = jnp.repeat(bias_vector, YL)[:, None]
    modes_shape = jax.ShapeDtypeStruct((CHUNKS, 64, KZT), BF)

    def unpack(modes):
        return modes.reshape(CHUNKS, 4, CC, 2, 2, KZT).transpose(1, 4, 0, 2, 3, 5).reshape(
            4, 2, C, 2, KZT
        )

    def pack(modes):
        return modes.reshape(4, 2, CHUNKS, CC, 2, KZT).transpose(2, 0, 3, 4, 1, 5).reshape(
            CHUNKS, 64, KZT
        )

    modes = pl.pallas_call(
        first_kernel,
        out_shape=modes_shape,
        in_specs=[ANY, VM, VM, VM],
        out_specs=VM,
        scratch_shapes=[
            pltpu.VMEM((CHUNKS, XL, CR, NZT), BF),
            pltpu.SemaphoreType.DMA((CHUNKS,)),
        ]
        + FORWARD_SCRATCH,
        compiler_params=params(1),
        name="first",
    )(grid, depth, yf, xf)
    spectral_modes = unpack(modes)

    def contract(weights, values):
        return jnp.einsum("abiok,abik->abok", weights, values, preferred_element_type=F32)

    def adjoint(weights, values):
        return jnp.einsum("abiok,abok->abik", weights, values, preferred_element_type=F32)

    weight_real = spectral_weight[:, :, :, :, 0]
    weight_imag = spectral_weight[:, :, :, :, 1]
    mode_real = spectral_modes[:, :, :, 0]
    mode_imag = spectral_modes[:, :, :, 1]
    real_sum = contract(weight_real, mode_real) - contract(weight_imag, mode_imag)
    imag_sum = contract(weight_real, mode_imag) + contract(weight_imag, mode_real)
    spectrum = (jnp.stack([real_sum, imag_sum], 3) * weights_mode).astype(BF)

    pre_grad, grad_modes = pl.pallas_call(
        second_kernel,
        out_shape=[jax.ShapeDtypeStruct((XL, ROWS, NZT), BF), modes_shape],
        in_specs=[ANY, ANY] + [VM] * 9,
        out_specs=[ANY, VM],
        scratch_shapes=[
            pltpu.VMEM((XL, ROWS, NZT), BF),
            pltpu.VMEM((CHUNKS, XL, CR, NZT), BF),
            pltpu.VMEM((CHUNKS, XL, CR, NZT), BF),
            pltpu.VMEM((XL, ROWS, NZT), F32),
            pltpu.SemaphoreType.DMA,
            pltpu.SemaphoreType.DMA((CHUNKS,)),
            pltpu.SemaphoreType.DMA((CHUNKS,)),
        ]
        + INVERSE_SCRATCH
        + FORWARD_SCRATCH,
        compiler_params=params(2),
        name="second",
    )(grid, cot, pack(spectrum), mixer_forward, bias_rows, depth, back, yf, yi, xf, xi)

    scaled = unpack(grad_modes) * weights_mode.astype(BF)
    scaled_real = scaled[:, :, :, 0]
    scaled_imag = scaled[:, :, :, 1]
    back_real = adjoint(weight_real, scaled_real) + adjoint(weight_imag, scaled_imag)
    back_imag = adjoint(weight_real, scaled_imag) - adjoint(weight_imag, scaled_real)
    grad_spectrum = jnp.stack([back_real, back_imag], 3).astype(BF)
    real_modes = mode_real.astype(F32)
    imag_modes = mode_imag.astype(F32)
    real_scaled = scaled_real.astype(F32)
    imag_scaled = scaled_imag.astype(F32)
    grad_real = (
        real_modes[:, :, :, None] * real_scaled[:, :, None]
        + imag_modes[:, :, :, None] * imag_scaled[:, :, None]
    )
    grad_imag = (
        real_modes[:, :, :, None] * imag_scaled[:, :, None]
        - imag_modes[:, :, :, None] * real_scaled[:, :, None]
    )
    spectral_grad = jnp.stack([grad_real, grad_imag], 4)

    fold = (jnp.arange(ROWS)[:, None] // YL == jnp.arange(128)[None, :]).astype(F32)
    input_grad, small = pl.pallas_call(
        third_kernel,
        out_shape=[
            jax.ShapeDtypeStruct((XL, ROWS, NZT), BF),
            jax.ShapeDtypeStruct((24, 128), F32),
        ],
        in_specs=[ANY, ANY] + [VM] * 6,
        out_specs=[ANY, VM],
        scratch_shapes=[
            pltpu.VMEM((XL, ROWS, NZT), BF),
            pltpu.VMEM((XL, ROWS, NZT), BF),
            pltpu.VMEM((CHUNKS, XL, CR, NZT), BF),
            pltpu.VMEM((XL, ROWS, NZT), F32),
            pltpu.VMEM((ROWS + 8, ROWS), F32),
            pltpu.VMEM((24, 128), F32),
            pltpu.VMEM((GX, 24, 128), F32),
            pltpu.VMEM((24, 128), F32),
            pltpu.VMEM((GY, 24, 128), F32),
            pltpu.SemaphoreType.DMA,
            pltpu.SemaphoreType.DMA,
            pltpu.SemaphoreType.DMA((CHUNKS,)),
            pltpu.SemaphoreType.DMA((4,)),
        ]
        + INVERSE_SCRATCH,
        compiler_params=params(3),
        name="third",
    )(grid, pre_grad, pack(grad_spectrum), mixer_back, fold, back, yi, xi)
    input_grad = jnp.swapaxes(input_grad.reshape(XL, C, YL, NZT), 1, 2)
    scale_factor = 1.0 / math.sqrt(NX * NY * NZT)
    small = small * scale_factor
    return (input_grad, spectral_grad, small[:C, :C], small[C, :C])


def solution(mesh):
    return jax.shard_map(
        body,
        mesh=mesh,
        in_specs=(
            P("gx", "gy", None, None),
            P("gx", "gy", None, None),
            P("gx", "gy", None, None, None, None),
            P(),
            P(),
        ),
        out_specs=(P("gx", "gy", None, None), P("gx", "gy", None, None, None, None), P(), P()),
        check_vma=False,
    )
```

time: 923 us -> 334 us (0.36); the launches traced: 913 us -> 334 us
  waiting for transfers between devices: 537 us -> 0 us
  Pallas kernels: 0 us -> 256 us
  matrix products: 125 us -> 0 us
  blocking collectives: 82.4 us -> 0 us
  local copies, waits for them, and re-layouts: 94.2 us -> 33.6 us
  between operations: 15.8 us -> 0.89 us
  other arithmetic: 58 us -> 44 us
    pallas_call x0 -> x3, Pallas kernels: none -> 256 us  [the longest x1 118 us: body(): pl.pallas_call(second_kernel, out_shape=[jax.ShapeDtypeStruct((XL, ROWS,...]
    reduce_scatter x2 -> x0, waiting for transfers between devices: 223 us -> none  [spectral_forward(): lax.psum_scatter(jnp.einsum('lpyq,xycqk->lxcpk', window, depth_modes, pre...]
    all_gather x4 -> x0, waiting for transfers between devices: 167 us -> none  [the longest x2 85.4 us: spectral_inverse(): lax.all_gather(inverse_x, 'gy', axis=1, tiled=True)]
    unnamed x10 -> x0, waiting for transfers between devices: 147 us -> none
    dot_general x15 -> x0, matrix products: 125 us -> none  [the longest x2 44.7 us: spectral_inverse(): jnp.einsum('lqyp,xlcqk->xycpk', window, lax.all_gather(inverse_x, 'gy', a...]
    psum x1 -> x0, blocking collectives: 82.4 us -> none  [body(): mixer_total, bias_total = lax.psum((mixer_local, bias_local), ('gx', 'gy'))]
    convert_element_type x6 -> x2, local copies, waits for them, and re-layouts: 31.4 us -> 0.04 us  [the longest x1 0.02 us: body(): imag_scaled = scaled_imag.astype(F32)]
    unnamed x5 -> x0, other arithmetic: 22 us -> none
  transfers between devices with their start and end apart: 8 -> 0, of which waited for: 7 -> 0; matrix products, arithmetic and copies ran while one was open for 5% -> 0% of each run, Pallas kernels for 0% -> 0%
where the time goes in v1:
time: 334 us
  Pallas kernels  256 us (77%)
  other arithmetic  44 us (13%)
  local copies, waits for them, and re-layouts  33.6 us (10%)
    pallas_call x1, Pallas kernels, body(): pl.pallas_call(second_kernel, out_shape=[jax.ShapeDtypeStruct((XL, ROWS,...  118 us
    pallas_call x1, Pallas kernels, body(): pl.pallas_call(third_kernel, out_shape=[jax.ShapeDtypeStruct((XL, ROWS, N...  74.7 us
    pallas_call x1, Pallas kernels, body(): pl.pallas_call(first_kernel, out_shape=modes_shape, in_specs=[ANY, VM, VM...  62.7 us
    dot_general x1, other arithmetic, contract(): jnp.einsum('abiok,abik->abok', weights, values, preferred_element_type=F32)  12.9 us
    another operation x1, other arithmetic, body(): spectral_grad = jnp.stack([grad_real, grad_imag], 4)  10.5 us
    slice x1, local copies, waits for them, and re-layouts, body(): weight_real = spectral_weight[:, :, :, :, 0]  8.89 us
    add x1, other arithmetic, body(): real_modes[:, :, :, None] * real_scaled[:, :, None]  8.61 us
    dot_general x1, other arithmetic, adjoint(): jnp.einsum('abiok,abok->abik', weights, values, preferred_element_type=F32)  7.3 us

profile of v1, /device:TPU:1, one launch (start us, length us, event | category | flops | bytes accessed | tf_op | source)
XLA Modules:
  0.0 334.0 jit_solution(14565728994848890040)
XLA Ops:
  0.7 1.7 dynamic-slice_bitcast_fusion.3.yf
  2.3 1.9 dynamic-slice_bitcast_fusion.xf
  4.2 62.7 %first.1 = bf16[5,64,256]{2,1,0:T(8,128)(2,1)} custom-call(bf16[16,160,1024]{2,1,0:T(8,128)(2,1)} %bitcast.116, bf16[1024,512]{1,0:T(8,128)(2,1)} %constant.85.clone.depth, bf16[256,512]{1,0:T(8,128)(2,1)} %dynamic-slice_bitcast_fusion.3.yf, bf16[512,512]{1,0:T(8,128)(2,1)} %dynamic-slice_bitcast_fusion.xf), custom_call_target="tpu_custom_call" | custom-call | tf_op jit(solution)/shard_map/first/pallas_call | solution.py:508
  66.9 1.0 reshape.134
  67.9 0.1 copy.24
  68.1 0.2 fusion.15
  68.3 1.0 bitcast_convert_fusion.5
  69.3 0.0 copy-done
  69.3 8.9 %fusion.13 = (bf16[4,2,20,20,1,256]{5,4,3,2,1,0:T(2,128)(2,1)}, bf16[4,2,20,20,1,256]{5,4,3,2,1,0:T(2,128)(2,1)}) fusion(bf16[4,2,20,20,2,256]{5,4,3,2,1,0:T(2,128)(2,1)S(1)} %copy-done), kind=kLoop, calls=%fused_computation.53 | loop fusion | bytes 6553600 | tf_op jit(solution)/shard_map/slice | solution.py:529
  78.2 12.9 %fusion = (f32[4,2,256,20]{2,1,3,0:T(2,128)S(1)}, f32[4,2,256,20]{2,1,3,0:T(2,128)S(1)}, f32[4,2,256,20]{2,1,3,0:T(2,128)S(1)}, f32[4,2,256,20]{2,1,3,0:T(2,128)...) fusion(f32[4,2,256,20]{2,1,3,0:T(2,128)} %get-tuple-element.46, ...), kind=kLoop, calls=%fused_computation.9 | loop fusion | flops 8028160 | bytes 7536640 | tf_op jit(solution)/shard_map/abiok,abik->abok/dot_general | solution.py:524
  91.1 0.1 add.58
  91.2 0.0 copy-start.7
  91.2 0.1 sub.33
  91.3 0.2 fusion.9
  91.4 0.1 copy.29
  91.6 0.7 reshape.136.spec
  92.3 0.0 copy-done.6
  92.3 1.1 multiply_bitcast_fusion
  93.5 1.5 copy.30
  95.0 2.4 reshape.137.mixer
  97.4 0.0 copy-done.7
  97.4 0.1 broadcast_in_dim.12
  97.5 0.7 broadcast_in_dim_reshape.4.bias
  98.2 1.7 dynamic-slice_bitcast_fusion.2.yi
  99.9 1.7 dynamic-slice_bitcast_fusion.1.xi
  101.5 118.1 %second.1 = (bf16[16,160,1024]{2,1,0:T(8,128)(2,1)}, bf16[5,64,256]{2,1,0:T(8,128)(2,1)}) custom-call(bf16[16,160,1024]{2,1,0:T(8,128)(2,1)} %bitcast.117, bf16[16,160,1024]{2,1,0:T(8,128)(2,1)} %bitcast.119, bf16[5,64,256]{2,1,0:T(8,128)(2,1)} %reshape.136.spec, bf16[160,160]{1,0:T(8,128)(2,1)} %reshape.137.mixer, f32[160,1]{1,0:T(8,128)} %broadcast_in_dim_reshape.4.bias, ...), custom_call_target="tpu_custom_call" | custom-call | tf_op jit(solution)/shard_map/second/pallas_call | solution.py:537
  219.6 1.0 reshape.138
  220.6 0.1 copy.32
  220.7 0.1 broadcast_multiply_fusion
  220.9 0.2 fusion.14
  221.1 0.1 bitcast_convert_fusion.3
  221.3 0.8 bitcast_convert_fusion.1
  222.1 7.3 %fusion.4 = (f32[4,2,256,20]{2,1,3,0:T(2,128)S(1)}, f32[4,2,256,20]{2,1,3,0:T(2,128)S(1)}, f32[4,2,256,20]{2,1,3,0:T(2,128)S(1)}, f32[4,2,256,20]{2,1,3,0:T(2,128)S(1)}) fusion(f32[4,2,256,20]{2,1,3,0:T(2,128)S(1)} %get-tuple-element.33, bf16[4,2,20,20,1,256]{5,1,3,2,0,4:T(2,128)(2,1)S(1)} %get-tuple-element.25, f32[4,2,256,20]{2,1,3,0:T(2,128)S(1)} %get-tuple-element.37, ...), kind=kLoop, calls=%fused_computation.13 | loop fusion | flops 8028160 | bytes 4259840 | tf_op jit(solution)/shard_map/abiok,abok->abik/dot_general | solution.py:527
  229.4 0.1 subtract_convert_fusion
  229.5 0.1 add_convert_fusion
  229.6 0.2 maximum_bitcast_fusion
  229.8 0.1 copy.35
  229.9 0.7 reshape.140.spec
  230.6 2.4 reshape.141.mixer
  233.1 0.7 fusion.10.fold
  233.8 74.7 %third.1 = (bf16[16,160,1024]{2,1,0:T(8,128)(2,1)}, f32[24,128]{1,0:T(8,128)}) custom-call(bf16[16,160,1024]{2,1,0:T(8,128)(2,1)} %bitcast.118, bf16[16,160,1024]{2,1,0:T(8,128)(2,1)} %get-tuple-element.8.grad_hbm, bf16[5,64,256]{2,1,0:T(8,128)(2,1)} %reshape.140.spec, bf16[160,160]{1,0:T(8,128)(2,1)} %reshape.141.mixer, f32[160,128]{1,0:T(8,128)} %fusion.10.fold, ...), custom_call_target="tpu_custom_call" | custom-call | tf_op jit(solution)/shard_map/third/pallas_call | solution.py:578
  308.6 0.0 copy-done.1
  308.7 0.0 copy-done.2
  308.7 8.6 %multiply_add_fusion = (f32[4,2,20,20,1,256]{5,4,3,2,1,0:T(1,128)S(1)}, f32[4,2,20,20,1,256]{5,4,3,2,1,0:T(1,128)}) fusion(f32[4,2,20,256]{3,2,1,0:T(8,128)S(1)} %copy.39, f32[4,2,20,256]{3,2,1,0:T(8,128)S(1)} %copy.38, f32[4,2,20,256]{3,2,1,0:T(8,128)S(1)} %copy.37, f32[4,2,20,256]{3,2,1,0:T(8,128)S(1)} %copy.36), kind=kLoop, calls=%fused_computation.18 | loop fusion | flops 4915200 | bytes 7208960 | tf_op jit(solution)/shard_map/add | solution.py:568
  317.3 10.5 %pad_maximum_fusion = f32[4,2,20,20,2,256]{5,4,3,2,1,0:T(2,128)} fusion(f32[4,2,20,20,1,256]{5,4,3,2,1,0:T(1,128)} %get-tuple-element.29, f32[4,2,20,20,1,256]{5,4,3,2,1,0:T(1,128)S(1)} %get-tuple-element.28), kind=kLoop, calls=%fused_computation | loop fusion | flops 1638400 | bytes 13107200 | tf_op jit(solution)/shard_map/stack | solution.py:575
  327.8 0.0 copy-done.4
  327.8 0.5 slice_bitcast_fusion
  328.4 5.6 %copy.127 = bf16[16,8,20,1024]{3,1,2,0:T(8,128)(2,1)} copy(bf16[16,8,20,1024]{3,1,2,0:T(8,128)(2,1)} %bitcast.120) | data formatting | bytes 10485760
  (17 shorter events, 0.1 us)
Async XLA Ops:
  4.2 65.1 %copy-start = (bf16[4,2,20,20,2,256]{5,4,3,2,1,0:T(2,128)(2,1)S(1)}, bf16[4,2,20,20,2,256]{5,4,3,2,1,0:T(2,128)(2,1)}, u32[]{:S(2)}) copy-start(bf16[4,2,20,20,2,256]{5,4,3,2,1,0:T(2,128)(2,1)} %param.13) | copy-start | bytes 9830404
  78.2 14.1 %copy-start.6 = (bf16[20,20]{1,0:T(8,128)(2,1)S(1)}, bf16[20,20]{1,0:T(8,128)(2,1)}, u32[]{:S(2)}) copy-start(bf16[20,20]{1,0:T(8,128)(2,1)} %param.14) | copy-start | bytes 2404
  91.2 6.2 %copy-start.7 = (f32[20]{0:T(128)S(1)}, f32[20]{0:T(128)}, u32[]{:S(2)}) copy-start(f32[20]{0:T(128)} %param.15) | copy-start | bytes 244
  233.8 74.8 %copy-start.1 = (f32[4,2,20,256]{3,1,2,0:T(2,128)S(1)}, f32[4,2,20,256]{3,1,2,0:T(2,128)}, u32[]{:S(2)}) copy-start(f32[4,2,20,256]{3,1,2,0:T(2,128)} %get-tuple-element.36) | copy-start | bytes 491524
  233.8 74.8 %copy-start.3 = (f32[4,2,20,256]{3,1,2,0:T(2,128)S(1)}, f32[4,2,20,256]{3,1,2,0:T(2,128)}, u32[]{:S(2)}) copy-start(f32[4,2,20,256]{3,1,2,0:T(2,128)} %get-tuple-element.34) | copy-start | bytes 491524
  233.8 74.8 %copy-start.2 = (f32[4,2,20,256]{3,1,2,0:T(2,128)S(1)}, f32[4,2,20,256]{3,1,2,0:T(2,128)}, u32[]{:S(2)}) copy-start(f32[4,2,20,256]{3,1,2,0:T(2,128)} %get-tuple-element.47) | copy-start | bytes 491524
  317.3 10.5 %copy-start.4 = (f32[24,128]{1,0:T(8,128)S(1)}, f32[24,128]{1,0:T(8,128)}, u32[]{:S(2)}) copy-start(f32[24,128]{1,0:T(8,128)} %get-tuple-element.11) | copy-start | bytes 36868
  327.8 6.2 %copy-start.5 = (f32[24,128]{1,0:T(8,128)}, f32[24,128]{1,0:T(8,128)S(1)}, u32[]{:S(2)}) copy-start(f32[24,128]{1,0:T(8,128)S(1)} %broadcast_multiply_fusion.1) | copy-start | bytes 36868

commit v2 on v1

v2 whole, which is shorter than its diff:
```python
import functools
import math

import jax
import jax.numpy as jnp
import ml_dtypes
import numpy as np
from jax import lax
from jax.experimental import pallas as pl
from jax.experimental.pallas import tpu as pltpu
from jax.sharding import PartitionSpec as P

NX = 128
NY = 128
NZ = 64
NT = 16
C = 20
MZ = 16
MT = 8
KX = 32
KY = 32
KZT = 256
NZT = 1024
GX = 8
GY = 16
HALF = 8
XL = NX // GX
YL = NY // GY
CHUNKS = 5
CC = C // CHUNKS
ROWS = C * YL
CR = CC * YL
BF = jnp.bfloat16
F32 = jnp.float32
MESH = pl.DeviceIdType.MESH


def signed_frequency(number):
    values = np.arange(number)
    return np.where(values < number // 2, values, values - number)


def pair_table(frequency, length):
    places = np.arange(length)
    phases = np.mod(frequency[:, None] * places[None, :], length)
    angles = phases * (-2.0 * math.pi / length)
    factor = float(length) ** (-0.5)
    cosine = np.cos(angles) * factor
    sine_part = np.sin(angles) * factor
    top_rows = np.stack([cosine, -sine_part], -1)
    low_rows = np.stack([sine_part, cosine], -1)
    return np.stack([top_rows, low_rows], 1)


def depth_table():
    fz = signed_frequency(2 * MZ)
    ft = np.arange(MT)
    z = np.arange(NZ)
    t = np.arange(NT)
    phases = (
        z[:, None, None, None] * fz[None, None, :, None] * NT
        + t[None, :, None, None] * ft[None, None, None, :] * NZ
    )
    phases = np.mod(phases, NZT).reshape(NZT, KZT)
    angles = phases * (-2.0 * math.pi / NZT)
    factor = float(NZT) ** (-0.5)
    stacked = np.stack([np.cos(angles) * factor, np.sin(angles) * factor], 1)
    return stacked.reshape(NZT, 2 * KZT)


def as_bf16(table):
    return np.ascontiguousarray(table).astype(np.float32).astype(ml_dtypes.bfloat16)


@functools.lru_cache(maxsize=None)
def tables():
    depth = depth_table()
    xt = pair_table(signed_frequency(KX), NX)
    yt = pair_table(signed_frequency(KY), NY)
    eye_c = np.eye(CC)
    eye_l = np.eye(2)
    yv = yt.reshape(GY, 2, 2, 2, HALF, YL, 2)
    yf = np.einsum("jlphsyq,cd->hjlcpsdqy", yv, eye_c).reshape(2, 256, 512)
    xv = xt.reshape(GX, 4, 2, GX, HALF, 2, 2)
    xf = np.einsum("iapgsxq,cd,lm->gialcpsxmdq", xv, eye_c, eye_l).reshape(GX, 512, 256)
    xi = np.transpose(xf, (0, 2, 1))
    yi = np.transpose(yf, (0, 2, 1))
    return tuple(as_bf16(v) for v in (depth, depth.T, yf, yi, xf, xi))


def mode_weight(shape):
    lanes = lax.broadcasted_iota(jnp.int32, shape, len(shape) - 1)
    return jnp.where(lax.rem(lanes, MT) == 0, 1.0, 2.0).astype(F32)


def gelu_slope(values):
    normal_cdf = 0.5 * (1.0 + lax.erf(values * (1.0 / math.sqrt(2.0))))
    density = jnp.exp(-0.5 * values * values) * (1.0 / math.sqrt(2.0 * math.pi))
    return normal_cdf + values * density


def mm(a, b):
    return jnp.dot(a, b, preferred_element_type=F32)


class Place:
    def __init__(self):
        self.gx = lax.axis_index("gx")
        self.gy = lax.axis_index("gy")
        self.lo = lax.rem(self.gy, HALF)
        self.hi = lax.div(self.gy, HALF)

    def x_peer(self, d):
        return lax.rem(self.gx + d, GX)

    def y_peer(self, d):
        return lax.rem(self.gy + d, GY)

    def half_peer(self, d):
        return lax.rem(self.lo + d, HALF)

    def greet(self):
        barrier = pltpu.get_barrier_semaphore()
        for d in range(1, GX):
            pl.semaphore_signal(
                barrier, inc=1, device_id={"gx": self.x_peer(d)}, device_id_type=MESH
            )
        for d in range(1, GY):
            pl.semaphore_signal(
                barrier, inc=1, device_id={"gy": self.y_peer(d)}, device_id_type=MESH
            )
        pl.semaphore_wait(barrier, GX + GY - 2)


def remote(src, dst, send, recv, device):
    pltpu.make_async_remote_copy(
        src_ref=src, dst_ref=dst, send_sem=send, recv_sem=recv,
        device_id=device, device_id_type=MESH,
    ).start()


def local(src, dst, sem):
    pltpu.make_async_copy(src, dst, sem).start()


def wait_for(region, sem):
    pltpu.make_async_copy(region, region, sem).wait()


def half_exchange(me, src, dst, send, recv):
    for d in range(1, HALF):
        peer = me.half_peer(d)
        remote(src.at[peer], dst.at[me.lo], send, recv, {"gy": me.hi * HALF + peer})
    local(src.at[me.lo], dst.at[me.lo], recv)


def twin(me, src, dst, send, recv):
    remote(src, dst, send, recv, {"gy": (1 - me.hi) * HALF + me.lo})


def column_exchange(me, src, dst, send, recv):
    for d in range(1, GX):
        peer = me.x_peer(d)
        remote(src.at[peer], dst.at[me.gx], send, recv, {"gx": peer})
    local(src.at[me.gx], dst.at[me.gx], recv)


def column_spread(me, src, dst, send, recv):
    for d in range(1, GX):
        remote(src, dst.at[me.gx], send, recv, {"gx": me.x_peer(d)})
    local(src, dst.at[me.gx], recv)


FORWARD_SCRATCH = [
    pltpu.VMEM((CHUNKS, HALF, 128, KZT), BF),
    pltpu.VMEM((CHUNKS, HALF, 128, KZT), BF),
    pltpu.VMEM((CHUNKS, 2, HALF, 32, KZT), BF),
    pltpu.VMEM((CHUNKS, HALF, 32, KZT), BF),
    pltpu.VMEM((CHUNKS, HALF, 32, KZT), BF),
    pltpu.VMEM((CHUNKS, HALF, 32, KZT), BF),
    pltpu.VMEM((CHUNKS, GX, 64, KZT), BF),
    pltpu.VMEM((CHUNKS, GX, 64, KZT), BF),
    pltpu.SemaphoreType.DMA((4, CHUNKS)),
    pltpu.SemaphoreType.DMA((4, CHUNKS)),
]
INVERSE_SCRATCH = [
    pltpu.VMEM((CHUNKS, GX, 64, KZT), BF),
    pltpu.VMEM((CHUNKS, HALF, 32, KZT), BF),
    pltpu.VMEM((CHUNKS, 2, HALF, 32, KZT), BF),
    pltpu.VMEM((CHUNKS, HALF, 128, KZT), BF),
    pltpu.VMEM((CHUNKS, HALF, 128, KZT), BF),
    pltpu.SemaphoreType.DMA((4, CHUNKS)),
    pltpu.SemaphoreType.DMA((4, CHUNKS)),
]


class Forward:
    def __init__(self, me, depth, yf, xf, out, sa, ra, half, other, sb, rb, sc, rc, send, recv):
        self.me, self.depth, self.yf, self.xf, self.out = me, depth, yf, xf, out
        self.sa, self.ra, self.sb, self.rb, self.sc, self.rc = sa, ra, sb, rb, sc, rc
        self.half, self.other = half, other
        self.send, self.recv = send, recv

    def put(self, c, part, parts, grid):
        count = XL // parts
        modes = mm(grid, self.depth[...])
        real = modes[:, :KZT].reshape(count, CC, 1, YL, KZT)
        imag = modes[:, KZT:].reshape(count, CC, 1, YL, KZT)
        both = jnp.concatenate([real, imag], 2).reshape(count * 64, KZT).astype(BF)
        self.sa[c, pl.ds(part * (count // 2), count // 2)] = both.reshape(count // 2, 128, KZT)

    def send_a(self, c):
        half_exchange(
            self.me, self.sa.at[c], self.ra.at[c], self.send.at[0, c], self.recv.at[0, c]
        )

    def stage_b(self, c):
        wait_for(self.ra.at[c], self.recv.at[0, c])
        for x2 in range(2):
            block = self.ra[c, :, x2 * 64 : x2 * 64 + 64, :].reshape(512, KZT)
            self.half[c, :, :, x2 * 16 : x2 * 16 + 16, :] = (
                mm(self.yf[...], block).astype(BF).reshape(2, HALF, 16, KZT)
            )
        twin(
            self.me, self.half.at[c, 1 - self.me.hi], self.other.at[c],
            self.send.at[1, c], self.recv.at[1, c],
        )

    def stage_e(self, c):
        wait_for(self.other.at[c], self.recv.at[1, c])
        mine = self.half[c, pl.ds(self.me.hi, 1)].reshape(HALF, 32, KZT)
        self.sb[c] = (mine.astype(F32) + self.other[c].astype(F32)).astype(BF)
        half_exchange(
            self.me, self.sb.at[c], self.rb.at[c], self.send.at[2, c], self.recv.at[2, c]
        )

    def stage_c(self, c):
        wait_for(self.rb.at[c], self.recv.at[2, c])
        block = self.rb[c].reshape(256, KZT)
        self.sc[c] = mm(self.xf[...], block).astype(BF).reshape(GX, 64, KZT)
        column_exchange(
            self.me, self.sc.at[c], self.rc.at[c], self.send.at[3, c], self.recv.at[3, c]
        )

    def stage_d(self, c):
        wait_for(self.rc.at[c], self.recv.at[3, c])
        total = self.rc[c, 0].astype(F32)
        for source in range(1, GX):
            total = total + self.rc[c, source].astype(F32)
        for half in range(2):
            lanes = slice(half * 128, half * 128 + 128)
            self.out[c, :, half] = total[:, lanes].reshape(8, 8, 128)

    def finish(self):
        @pl.loop(0, CHUNKS)
        def _(c):
            wait_for(self.sa.at[c, pl.ds(0, HALF - 1)], self.send.at[0, c])
            wait_for(self.other.at[c], self.send.at[1, c])
            wait_for(self.sb.at[c, pl.ds(0, HALF - 1)], self.send.at[2, c])
            wait_for(self.sc.at[c, pl.ds(0, GX - 1)], self.send.at[3, c])


class Inverse:
    def __init__(self, me, back, yi, xi, spec, rp, sq, rq, sr, rr, send, recv):
        self.me, self.back, self.yi, self.xi, self.spec = me, back, yi, xi, spec
        self.rp, self.sq, self.rq, self.sr, self.rr = rp, sq, rq, sr, rr
        self.send, self.recv = send, recv

    def stage_p(self, c):
        column_spread(
            self.me, self.spec.at[c], self.rp.at[c], self.send.at[0, c], self.recv.at[0, c]
        )

    def stage_q(self, c):
        wait_for(self.rp.at[c], self.recv.at[0, c])
        block = self.rp[c].reshape(512, KZT)
        self.sq[c] = mm(self.xi[...], block).astype(BF).reshape(HALF, 32, KZT)
        half_exchange(
            self.me, self.sq.at[c], self.rq.at[c, self.me.hi],
            self.send.at[1, c], self.recv.at[1, c],
        )

    def stage_t(self, c):
        mine = self.rq.at[c, self.me.hi]
        wait_for(mine, self.recv.at[1, c])
        twin(self.me, mine, mine, self.send.at[2, c], self.recv.at[2, c])

    def stage_r(self, c):
        wait_for(self.rq.at[c, 1 - self.me.hi], self.recv.at[2, c])
        for x2 in range(2):
            block = self.rq[c, :, :, x2 * 16 : x2 * 16 + 16, :].reshape(256, KZT)
            self.sr[c, :, x2 * 64 : x2 * 64 + 64, :] = (
                mm(self.yi[...], block).astype(BF).reshape(HALF, 64, KZT)
            )
        half_exchange(
            self.me, self.sr.at[c], self.rr.at[c], self.send.at[3, c], self.recv.at[3, c]
        )

    def ready(self, c):
        wait_for(self.rr.at[c], self.recv.at[3, c])

    def branch(self, c, part, parts):
        count = XL // parts
        block = self.rr[c, pl.ds(part * (count // 2), count // 2)].astype(F32)
        block = block.reshape(count, CC, 2, YL, KZT)
        real = block[:, :, 0].reshape(count * CR, KZT).astype(BF)
        imag = block[:, :, 1].reshape(count * CR, KZT).astype(BF)
        return mm(real, self.back[:KZT, :]) + mm(imag, self.back[KZT:, :])

    def finish(self):
        @pl.loop(0, CHUNKS)
        def _(c):
            wait_for(self.rp.at[c, pl.ds(0, GX - 1)], self.send.at[0, c])
            wait_for(self.sq.at[c, pl.ds(0, HALF - 1)], self.send.at[1, c])
            wait_for(self.sq.at[c], self.send.at[2, c])
            wait_for(self.sr.at[c, pl.ds(0, HALF - 1)], self.send.at[3, c])


def staged(stages, extras=()):
    depth = len(stages)

    @pl.loop(0, CHUNKS + depth - 1)
    def _(t):
        for s, stage in enumerate(stages):
            @pl.when(jnp.logical_and(t >= s, t < CHUNKS + s))
            def _(stage=stage, s=s):
                stage(t - s)
        for step, extra in extras:
            @pl.when(t == step)
            def _(extra=extra):
                extra()


TILES = 10
TILE = (TILES, 8, 128)


def tile_rows():
    return lax.broadcasted_iota(jnp.int32, (8, 128), 0)


def swap_parts(tiles):
    even = (lax.rem(lax.broadcasted_iota(jnp.int32, TILE, 1), 2) == 0)
    return jnp.where(even, pltpu.roll(tiles, 7, 1), pltpu.roll(tiles, 1, 1)), even


def coefficient(modes, kl, i, part):
    row = pl.ds((i % CC) * 2 + part, 1)
    low = jnp.broadcast_to(modes[i // CC, kl, 0, row, :], (8, 128))
    high = jnp.broadcast_to(modes[i // CC, kl, 1, row, :], (8, 128))
    return jnp.where(lax.rem(tile_rows(), 4) < 2, low, high)


def tiles_of(modes, kl, flat):
    for c in range(CHUNKS):
        for half in range(2):
            for part in range(2):
                flat[pl.ds(c * 16 + half * 2 + part, CC, 4), :] = modes[
                    c, kl, half, pl.ds(part, CC, 2), :
                ]
    return flat[...].reshape(TILE)


def pack_halves(values, out):
    for half in range(2):
        lanes = slice(half * 128, half * 128 + 128)
        out[:, :, lanes] = values[:, :, half].reshape(CHUNKS, 64, 128).astype(BF)


def mix_modes(modes, weight, flat, spec, out):
    @pl.loop(0, 8)
    def _(kl):
        by_real = jnp.zeros(TILE, F32)
        by_imag = jnp.zeros(TILE, F32)
        for i in range(C):
            block = weight[kl * C + i].astype(F32).reshape(TILE)
            by_real = by_real + block * coefficient(modes, kl, i, 0)[None]
            by_imag = by_imag + block * coefficient(modes, kl, i, 1)[None]
        turned, even = swap_parts(by_imag)
        flat[...] = (by_real + jnp.where(even, -turned, turned)).reshape(80, 128)
        for c in range(CHUNKS):
            for half in range(2):
                for part in range(2):
                    spec[c, kl, half, pl.ds(part, CC, 2), :] = flat[
                        pl.ds(c * 16 + half * 2 + part, CC, 4), :
                    ]

    pack_halves(spec[...] * mode_weight(spec.shape), out)


def adjoint_modes(scaled, weight, flat, sums, spec, out):
    @pl.loop(0, 8)
    def _(kl):
        grad = tiles_of(scaled, kl, flat)
        turned, even = swap_parts(grad)
        turned = jnp.where(even, turned, -turned)
        for i in range(C):
            block = weight[kl * C + i].astype(F32).reshape(TILE)
            sums[0, i * 8 : i * 8 + 8] = (block * grad).sum(0)
            sums[1, i * 8 : i * 8 + 8] = (block * turned).sum(0)
        for c in range(CHUNKS):
            for half in range(2):
                for part in range(2):
                    total = None
                    for row in (0, 1, 4, 5):
                        term = sums[part, pl.ds(c * 32 + half * 2 + row, CC, 8), :]
                        total = term if total is None else total + term
                    spec[c, kl, half, pl.ds(part, CC, 2), :] = total

    pack_halves(spec[...], out)


def gradient_kernel(modes, scaled, out, flat):
    kl = pl.program_id(0)
    grad = tiles_of(scaled, kl, flat)
    turned, even = swap_parts(grad)
    turned = jnp.where(even, turned, -turned)
    for i in range(C):
        real = coefficient(modes, kl, i, 0)[None]
        imag = coefficient(modes, kl, i, 1)[None]
        out[i] = (grad * real + turned * imag).reshape(80, 128)


def channel_rows():
    rows = lax.broadcasted_iota(jnp.int32, (ROWS, C), 0)
    return lax.div(rows, YL) == lax.broadcasted_iota(jnp.int32, (ROWS, C), 1)


def same_place():
    rows = lax.broadcasted_iota(jnp.int32, (ROWS, ROWS), 0)
    columns = lax.broadcasted_iota(jnp.int32, (ROWS, ROWS), 1)
    return lax.rem(rows, YL) == lax.rem(columns, YL)


def spread_mixer(mixer, axis):
    spread = jnp.where(channel_rows(), 1.0, 0.0).astype(BF)
    half = lax.dot_general(
        spread, mixer, (((1,), (1 - axis,)), ((), ())), preferred_element_type=F32
    ).astype(BF)
    full = lax.dot_general(
        half, spread, (((1,), (1,)), ((), ())), preferred_element_type=F32
    )
    return jnp.where(same_place(), full, 0.0).astype(BF)


FORWARD_TABLES = [
    pltpu.VMEM((NZT, 2 * KZT), BF),
    pltpu.VMEM((256, 512), BF),
    pltpu.VMEM((512, 256), BF),
    pltpu.SemaphoreType.DMA((3,)),
]
INVERSE_TABLES = [
    pltpu.VMEM((2 * KZT, NZT), BF),
    pltpu.VMEM((512, 256), BF),
    pltpu.VMEM((256, 512), BF),
    pltpu.SemaphoreType.DMA((3,)),
]


def fetch_tables(me, depth_hbm, y_hbm, x_hbm, depth, y, x, sem):
    pairs = ((depth_hbm, depth), (y_hbm.at[me.hi], y), (x_hbm.at[me.gx], x))
    for n, (src, dst) in enumerate(pairs):
        local(src, dst, sem.at[n])

    def ready():
        for n, (_, dst) in enumerate(pairs):
            wait_for(dst, sem.at[n])

    return ready


def load_chunks(src, dst, sem):
    @pl.loop(0, CHUNKS)
    def _(c):
        local(src.at[:, pl.ds(c * CR, CR), :], dst.at[c], sem.at[c])


def wait_chunks(dst, sem):
    @pl.loop(0, CHUNKS)
    def _(c):
        wait_for(dst.at[c], sem.at[c])


def first_kernel(
    x_hbm, weight_hbm, depth_hbm, yf_hbm, xf_hbm, modes, spec_out,
    xbuf, weight, flat, spec, xsem, wsem, depth, yf, xf, tsem, *scratch
):
    me = Place()
    load_chunks(x_hbm, xbuf, xsem)
    tables_ready = fetch_tables(me, depth_hbm, yf_hbm, xf_hbm, depth, yf, xf, tsem)
    local(weight_hbm, weight, wsem)
    me.greet()
    fwd = Forward(me, depth, yf, xf, modes, *scratch)
    tables_ready()

    def stage_a(c):
        wait_for(xbuf.at[c], xsem.at[c])
        for part in range(2):
            fwd.put(c, part, 2, xbuf[c, part * 8 : part * 8 + 8].reshape(8 * CR, NZT))
        fwd.send_a(c)

    staged([stage_a, fwd.stage_b, fwd.stage_e, fwd.stage_c, fwd.stage_d])
    wait_for(weight, wsem)
    mix_modes(modes, weight, flat, spec, spec_out)
    fwd.finish()


def second_kernel(
    x_hbm, cot_hbm, weight_hbm, spec_in, mixer, bias,
    depth_hbm, yf_hbm, xf_hbm, back_hbm, yi_hbm, xi_hbm,
    grad_hbm, scaled, spec_out,
    cbuf, gbuf, point, weight, flat, sums, spec, xsem, csem, gsem, wsem, *scratch
):
    me = Place()
    n = len(FORWARD_TABLES)
    depth, yf, xf, tsem, back, yi, xi, isem = scratch[: 2 * n]
    scratch = scratch[2 * n :]
    inverse_ready = fetch_tables(me, back_hbm, yi_hbm, xi_hbm, back, yi, xi, isem)
    load_chunks(x_hbm, gbuf, xsem)
    load_chunks(cot_hbm, cbuf, csem)
    forward_ready = fetch_tables(me, depth_hbm, yf_hbm, xf_hbm, depth, yf, xf, tsem)
    local(weight_hbm, weight, wsem)
    me.greet()
    n = len(INVERSE_SCRATCH)
    inv = Inverse(me, back, yi, xi, spec_in, *scratch[:n])
    fwd = Forward(me, depth, yf, xf, scaled, *scratch[n:])

    @pl.loop(0, CHUNKS)
    def _(c):
        inv.stage_p(c)

    inverse_ready()
    forward_ready()
    wait_chunks(gbuf, xsem)

    def pointwise(part):
        spread = spread_mixer(mixer[...], 0)
        shift = jnp.where(channel_rows(), bias[...], 0.0).sum(1, keepdims=True)

        @pl.loop(part * 8, part * 8 + 8)
        def _(x):
            point[x] = mm(spread, gbuf[:, x].reshape(ROWS, NZT)) + shift

    def stage_s(c):
        inv.ready(c)
        wait_for(cbuf.at[c], csem.at[c])

        @pl.loop(0, 2)
        def _(part):
            rows = pl.ds(part * 8, 8)
            pre = inv.branch(c, part, 2)
            pre = pre + point[rows, pl.ds(c * CR, CR), :].reshape(8 * CR, NZT)
            cot = cbuf[c, rows].reshape(8 * CR, NZT).astype(F32)
            grad = (cot * gelu_slope(pre)).astype(BF)
            gbuf[c, rows] = grad.reshape(8, CR, NZT)
            fwd.put(c, part, 2, grad)

        local(gbuf.at[c], grad_hbm.at[:, pl.ds(c * CR, CR), :], gsem.at[c])
        fwd.send_a(c)

    staged(
        [
            inv.stage_q, inv.stage_t, inv.stage_r, stage_s,
            fwd.stage_b, fwd.stage_e, fwd.stage_c, fwd.stage_d,
        ],
        [(0, lambda: pointwise(0)), (1, lambda: pointwise(1))],
    )
    scaled[...] = scaled[...] * mode_weight(scaled.shape)
    wait_for(weight, wsem)
    adjoint_modes(scaled, weight, flat, sums, spec, spec_out)
    wait_chunks(gbuf, gsem)
    inv.finish()
    fwd.finish()


def third_kernel(
    x_hbm, grad_hbm, spec_in, mixer, back_hbm, yi_hbm, xi_hbm, out_hbm, mixer_out, bias_out,
    xbuf, gbuf, obuf, point, mixed, one, col, two, row, xsem, gsem, osem, small, *scratch
):
    me = Place()
    n = len(INVERSE_TABLES)
    back, yi, xi, isem = scratch[:n]
    inverse_ready = fetch_tables(me, back_hbm, yi_hbm, xi_hbm, back, yi, xi, isem)
    local(x_hbm, xbuf, xsem)
    local(grad_hbm, gbuf, gsem)
    me.greet()
    inv = Inverse(me, back, yi, xi, spec_in, *scratch[n:])

    @pl.loop(0, CHUNKS)
    def _(c):
        inv.stage_p(c)

    inverse_ready()
    wait_for(xbuf, xsem)
    wait_for(gbuf, gsem)
    mixed[...] = jnp.zeros_like(mixed)

    def pointwise(part):
        spread = spread_mixer(mixer[...], 1)
        contract = (((1,), (1,)), ((), ()))

        @pl.loop(part * 8, part * 8 + 8)
        def _(x):
            grad = gbuf[x]
            point[x] = mm(spread, grad)
            mixed[:ROWS, :] += lax.dot_general(
                xbuf[x], grad, contract, preferred_element_type=F32
            )
            mixed[ROWS:, :] += lax.dot_general(
                jnp.ones((8, NZT), BF), grad, contract, preferred_element_type=F32
            )

    def second_half():
        pointwise(1)
        kept = jnp.where(same_place(), mixed[:ROWS, :], 0.0).reshape(C, YL, ROWS).sum(1)
        stacked = jnp.concatenate([kept, mixed[ROWS : ROWS + 4, :]], 0)
        fold = lax.div(lax.broadcasted_iota(jnp.int32, (ROWS, 128), 0), YL)
        fold = fold == lax.broadcasted_iota(jnp.int32, (ROWS, 128), 1)
        one[...] = lax.dot_general(
            stacked, jnp.where(fold, 1.0, 0.0), (((1,), (0,)), ((), ())),
            precision=lax.Precision.HIGHEST, preferred_element_type=F32,
        )
        for d in range(1, GX):
            remote(one, col.at[me.gx], small.at[0], small.at[1], {"gx": me.x_peer(d)})
        local(one, col.at[me.gx], small.at[1])

    def across_rows():
        wait_for(col, small.at[1])
        total = col[0]
        for source in range(1, GX):
            total = total + col[source]
        two[...] = total
        for d in range(1, GY):
            remote(two, row.at[me.gy], small.at[2], small.at[3], {"gy": me.y_peer(d)})
        local(two, row.at[me.gy], small.at[3])

    def stage_s(c):
        inv.ready(c)

        @pl.loop(0, 2)
        def _(part):
            rows = pl.ds(part * 8, 8)
            total = inv.branch(c, part, 2)
            total = total + point[rows, pl.ds(c * CR, CR), :].reshape(8 * CR, NZT)
            obuf[c, rows] = total.astype(BF).reshape(8, CR, NZT)

        local(obuf.at[c], out_hbm.at[:, pl.ds(c * CR, CR), :], osem.at[c])

    staged(
        [inv.stage_q, inv.stage_t, inv.stage_r, stage_s],
        [(0, lambda: pointwise(0)), (1, second_half), (3, across_rows)],
    )
    wait_for(row, small.at[3])
    total = row[0]
    for source in range(1, GY):
        total = total + row[source]
    total = total * (1.0 / math.sqrt(NX * NY * NZT))
    mixer_out[...] = total[:C, :C]
    bias_out[...] = total[C : C + 1, :C]
    wait_for(col.at[pl.ds(0, GX - 1)], small.at[0])
    wait_for(row.at[pl.ds(0, GY - 1)], small.at[2])
    wait_chunks(obuf, osem)
    inv.finish()


ANY = pl.BlockSpec(memory_space=pl.ANY)
VM = pl.BlockSpec(memory_space=pltpu.VMEM)


def params(number):
    return pltpu.CompilerParams(
        collective_id=number, has_side_effects=True, vmem_limit_bytes=60 * 2**20
    )


def body(layer_input, cotangent, spectral_weight, mixer_weight, bias_vector):
    depth, back, yf, yi, xf, xi = (jnp.asarray(v) for v in tables())
    grid = jnp.swapaxes(layer_input, 1, 2).reshape(XL, ROWS, NZT)
    cot = jnp.swapaxes(cotangent, 1, 2).reshape(XL, ROWS, NZT)
    weight = spectral_weight.reshape(8 * C, C, 2, 2, 128)
    weight = jnp.swapaxes(weight, 2, 3).reshape(8 * C, 4 * C, 128)
    modes_f32 = jax.ShapeDtypeStruct((CHUNKS, 8, 2, 8, 128), F32)
    modes_bf16 = jax.ShapeDtypeStruct((CHUNKS, 64, KZT), BF)
    field = jax.ShapeDtypeStruct((XL, ROWS, NZT), BF)
    chunked = pltpu.VMEM((CHUNKS, XL, CR, NZT), BF)
    chunk_sems = pltpu.SemaphoreType.DMA((CHUNKS,))
    weights_held = pltpu.VMEM((8 * C, 4 * C, 128), BF)
    flat = pltpu.VMEM((4 * C, 128), F32)
    spec_held = pltpu.VMEM((CHUNKS, 8, 2, 8, 128), F32)

    modes, spectrum = pl.pallas_call(
        first_kernel,
        out_shape=[modes_f32, modes_bf16],
        in_specs=[ANY] * 5,
        out_specs=[VM, VM],
        scratch_shapes=[
            chunked, weights_held, flat, spec_held, chunk_sems, pltpu.SemaphoreType.DMA,
        ]
        + FORWARD_TABLES
        + FORWARD_SCRATCH,
        compiler_params=params(1),
        name="first",
    )(grid, weight, depth, yf, xf)

    pre_grad, scaled, grad_spectrum = pl.pallas_call(
        second_kernel,
        out_shape=[field, modes_f32, modes_bf16],
        in_specs=[ANY, ANY, ANY] + [VM] * 3 + [ANY] * 6,
        out_specs=[ANY, VM, VM],
        scratch_shapes=[
            chunked, chunked, pltpu.VMEM((XL, ROWS, NZT), F32), weights_held, flat,
            pltpu.VMEM((2, 8 * C, 128), F32), spec_held,
            chunk_sems, chunk_sems, chunk_sems, pltpu.SemaphoreType.DMA,
        ]
        + FORWARD_TABLES
        + INVERSE_TABLES
        + INVERSE_SCRATCH
        + FORWARD_SCRATCH,
        compiler_params=params(2),
        name="second",
    )(
        grid, cot, weight, spectrum, mixer_weight, bias_vector.reshape(1, C),
        depth, yf, xf, back, yi, xi,
    )

    spectral_grad = pl.pallas_call(
        gradient_kernel,
        out_shape=jax.ShapeDtypeStruct((8 * C, 4 * C, 128), F32),
        grid=(8,),
        in_specs=[pl.BlockSpec((CHUNKS, 8, 2, 8, 128), lambda kl: (0, 0, 0, 0, 0))] * 2,
        out_specs=pl.BlockSpec((C, 4 * C, 128), lambda kl: (kl, 0, 0)),
        scratch_shapes=[flat],
        name="gradient",
    )(modes, scaled)
    spectral_grad = jnp.swapaxes(spectral_grad.reshape(8 * C, C, 2, 2, 128), 2, 3)
    spectral_grad = spectral_grad.reshape(4, 2, C, C, 2, KZT)

    input_grad, mixer_grad, bias_grad = pl.pallas_call(
        third_kernel,
        out_shape=[
            field, jax.ShapeDtypeStruct((C, C), F32), jax.ShapeDtypeStruct((1, C), F32),
        ],
        in_specs=[ANY, ANY, VM, VM] + [ANY] * 3,
        out_specs=[ANY, VM, VM],
        scratch_shapes=[
            pltpu.VMEM((XL, ROWS, NZT), BF),
            pltpu.VMEM((XL, ROWS, NZT), BF),
            chunked,
            pltpu.VMEM((XL, ROWS, NZT), F32),
            pltpu.VMEM((ROWS + 8, ROWS), F32),
            pltpu.VMEM((24, 128), F32),
            pltpu.VMEM((GX, 24, 128), F32),
            pltpu.VMEM((24, 128), F32),
            pltpu.VMEM((GY, 24, 128), F32),
            pltpu.SemaphoreType.DMA,
            pltpu.SemaphoreType.DMA,
            chunk_sems,
            pltpu.SemaphoreType.DMA((4,)),
        ]
        + INVERSE_TABLES
        + INVERSE_SCRATCH,
        compiler_params=params(3),
        name="third",
    )(grid, pre_grad, grad_spectrum, mixer_weight, back, yi, xi)
    input_grad = jnp.swapaxes(input_grad.reshape(XL, C, YL, NZT), 1, 2)
    return (input_grad, spectral_grad, mixer_grad, bias_grad.reshape(C))


def solution(mesh):
    return jax.shard_map(
        body,
        mesh=mesh,
        in_specs=(
            P("gx", "gy", None, None),
            P("gx", "gy", None, None),
            P("gx", "gy", None, None, None, None),
            P(),
            P(),
        ),
        out_specs=(P("gx", "gy", None, None), P("gx", "gy", None, None, None, None), P(), P()),
        check_vma=False,
    )
```

time: 334 us -> 244 us (0.73)
  other arithmetic: 44 us -> 0 us
  local copies, waits for them, and re-layouts: 33.6 us -> 6.77 us
  Pallas kernels: 256 us -> 236 us
    dot_general x2 -> x0, other arithmetic: 20.2 us -> none  [the longest x1 12.9 us: contract(): jnp.einsum('abiok,abik->abok', weights, values, preferred_element_type=F32)]
    pallas_call x3 -> x4, Pallas kernels: 256 us -> 236 us  [the longest x1 108 us: body(): pl.pallas_call(second_kernel, out_shape=[field, modes_f32, modes_bf16], i...]
    another operation x4 -> x0, other arithmetic: 10.7 us -> none  [the longest x1 10.5 us: body(): spectral_grad = jnp.stack([grad_real, grad_imag], 4)]
    slice x3 -> x0, local copies, waits for them, and re-layouts: 9.35 us -> none  [the longest x1 8.89 us: body(): weight_real = spectral_weight[:, :, :, :, 0]]
    add x2 -> x0, other arithmetic: 8.7 us -> none  [the longest x1 8.61 us: body(): real_modes[:, :, :, None] * real_scaled[:, :, None]]
    reshape x8 -> x0, local copies, waits for them, and re-layouts: 8.57 us -> none  [the longest x1 2.44 us: body(): jnp.einsum('io,yz->iyoz', mixer_weight, eye).reshape(ROWS, ROWS)]
    squeeze x5 -> x0, local copies, waits for them, and re-layouts: 7.43 us -> none  [the longest x1 1.88 us: body(): xf = lax.dynamic_index_in_dim(xf_all, gx, 0, False)]
    unnamed x17 -> x7, local copies, waits for them, and re-layouts: 5.66 us -> 6.77 us
where the time goes in v2:
time: 244 us; the launch traced here: 243 us
  Pallas kernels  236 us (97%)
  local copies, waits for them, and re-layouts  6.77 us (3%)
    pallas_call x1, Pallas kernels, body(): pl.pallas_call(second_kernel, out_shape=[field, modes_f32, modes_bf16], i...  108 us
    pallas_call x1, Pallas kernels, body(): pl.pallas_call(third_kernel, out_shape=[field, jax.ShapeDtypeStruct((C, C...  62.2 us
    pallas_call x1, Pallas kernels, body(): pl.pallas_call(first_kernel, out_shape=[modes_f32, modes_bf16], in_specs=...  60.9 us
    unnamed x7, local copies, waits for them, and re-layouts  6.77 us
    pallas_call x1, Pallas kernels, body(): pl.pallas_call(gradient_kernel, out_shape=jax.ShapeDtypeStruct((8 * C, 4...  5.4 us

profile of v2, /device:TPU:1, one launch (start us, length us, event | category | flops | bytes accessed | tf_op | source)
XLA Modules:
  0.0 243.4 jit_solution(11770121748196499319)
XLA Ops:
  0.6 60.9 %first.1 = (f32[5,8,2,8,128]{4,3,2,1,0:T(8,128)}, bf16[5,64,256]{2,1,0:T(8,128)(2,1)}) custom-call(bf16[16,160,1024]{2,1,0:T(8,128)(2,1)} %bitcast.21, bf16[160,80,128]{2,1,0:T(8,128)(2,1)} %bitcast.24, bf16[1024,512]{1,0:T(8,128)(2,1)} %constant.12.clone.depth_hbm, bf16[2,256,512]{2,1,0:T(8,128)(2,1)} %constant.14.clone.yf_hbm, ...), custom_call_target="tpu_custom_call" | custom-call | tf_op jit(solution)/shard_map/first/pallas_call | solution.py:691
  61.5 107.5 %second.1 = (bf16[16,160,1024]{2,1,0:T(8,128)(2,1)}, f32[5,8,2,8,128]{4,3,2,1,0:T(8,128)}, bf16[5,64,256]{2,1,0:T(8,128)(2,1)}) custom-call(bf16[16,160,1024]{2,1,0:T(8,128)(2,1)} %bitcast.22, bf16[16,160,1024]{2,1,0:T(8,128)(2,1)} %bitcast.28, bf16[160,80,128]{2,1,0:T(8,128)(2,1)} %bitcast.25, bf16[5,64,256]{2,1,0:T(8,128)(2,1)} %get-tuple-element.12.spec_in, ...), custom_call_target="tpu_custom_call" | custom-call | tf_op jit(solution)/shard_map/second/pallas_call | solution.py:705
  169.0 62.2 %third.1 = (bf16[16,160,1024]{2,1,0:T(8,128)(2,1)}, f32[20,20]{1,0:T(8,128)}, f32[1,20]{1,0:T(1,128)}) custom-call(bf16[16,160,1024]{2,1,0:T(8,128)(2,1)} %bitcast.23, bf16[16,160,1024]{2,1,0:T(8,128)(2,1)} %get-tuple-element.13.grad_hbm, bf16[5,64,256]{2,1,0:T(8,128)(2,1)} %get-tuple-element.14.spec_in, bf16[20,20]{1,0:T(8,128)(2,1)} %mixer.3, ...), custom_call_target="tpu_custom_call" | custom-call | tf_op jit(solution)/shard_map/third/pallas_call | solution.py:738
  231.3 5.4 %gradient.1 = f32[160,80,128]{2,1,0:T(8,128)} custom-call(f32[5,8,2,8,128]{4,3,2,1,0:T(8,128)} %get-tuple-element.16.modes, f32[5,8,2,8,128]{4,3,2,1,0:T(8,128)} %get-tuple-element.17.scaled), custom_call_target="tpu_custom_call" | custom-call | tf_op jit(solution)/shard_map/gradient/pallas_call | solution.py:726
  236.7 0.0 copy-start
  236.7 0.0 copy-start.1
  236.7 5.6 %copy.20 = bf16[16,8,20,1024]{3,1,2,0:T(8,128)(2,1)} copy(bf16[16,8,20,1024]{3,1,2,0:T(8,128)(2,1)} %bitcast.27) | data formatting | bytes 10485760
  242.3 0.0 copy-done
  242.3 0.6 copy.21
  242.9 0.0 copy-done.1
  242.9 0.5 copy.22
Async XLA Ops:
  236.7 5.7 %copy-start = (f32[20,20]{1,0:T(8,128)S(1)}, f32[20,20]{1,0:T(8,128)}, u32[]{:S(2)}) copy-start(f32[20,20]{1,0:T(8,128)} %get-tuple-element.26) | copy-start | bytes 4804
  236.7 6.3 %copy-start.1 = (f32[1,20]{1,0:T(1,128)S(1)}, f32[1,20]{1,0:T(1,128)}, u32[]{:S(2)}) copy-start(f32[1,20]{1,0:T(1,128)} %get-tuple-element.19) | copy-start | bytes 244

commit v3 on v2

v3 whole, which is shorter than its diff:
```python
import functools
import math

import jax
import jax.numpy as jnp
import ml_dtypes
import numpy as np
from jax import lax
from jax.experimental import pallas as pl
from jax.experimental.pallas import tpu as pltpu
from jax.sharding import PartitionSpec as P

NX = 128
NY = 128
NZ = 64
NT = 16
C = 20
MZ = 16
MT = 8
KX = 32
KY = 32
KZT = 256
NZT = 1024
GX = 8
GY = 16
HALF = 8
XL = NX // GX
YL = NY // GY
CHUNKS = 5
CC = C // CHUNKS
ROWS = C * YL
CR = CC * YL
BF = jnp.bfloat16
F32 = jnp.float32
MESH = pl.DeviceIdType.MESH


def signed_frequency(number):
    values = np.arange(number)
    return np.where(values < number // 2, values, values - number)


def pair_table(frequency, length):
    places = np.arange(length)
    phases = np.mod(frequency[:, None] * places[None, :], length)
    angles = phases * (-2.0 * math.pi / length)
    factor = float(length) ** (-0.5)
    cosine = np.cos(angles) * factor
    sine_part = np.sin(angles) * factor
    top_rows = np.stack([cosine, -sine_part], -1)
    low_rows = np.stack([sine_part, cosine], -1)
    return np.stack([top_rows, low_rows], 1)


def depth_table():
    fz = signed_frequency(2 * MZ)
    ft = np.arange(MT)
    z = np.arange(NZ)
    t = np.arange(NT)
    phases = (
        z[:, None, None, None] * fz[None, None, :, None] * NT
        + t[None, :, None, None] * ft[None, None, None, :] * NZ
    )
    phases = np.mod(phases, NZT).reshape(NZT, KZT)
    angles = phases * (-2.0 * math.pi / NZT)
    factor = float(NZT) ** (-0.5)
    stacked = np.stack([np.cos(angles) * factor, np.sin(angles) * factor], 1)
    return stacked.reshape(NZT, 2 * KZT)


def as_bf16(table):
    return np.ascontiguousarray(table).astype(np.float32).astype(ml_dtypes.bfloat16)


@functools.lru_cache(maxsize=None)
def tables():
    depth = depth_table()
    by_half = np.moveaxis(depth.reshape(NZT, 2, 2, 128), 2, 0).reshape(2, NZT, 256)
    xt = pair_table(signed_frequency(KX), NX)
    yt = pair_table(signed_frequency(KY), NY)
    eye = np.eye(2)
    yv = yt.reshape(GY, 2, 2, 2, HALF, YL, 2)
    yf = np.einsum("jlphsyq,cd,ab->hjalcpsbdqy", yv, eye, eye).reshape(2, 256, 512)
    xv = xt.reshape(GX, 4, 2, GX, HALF, 2, 2)
    xf = np.einsum("iapgsxq,cd,lm->gialcpsxmdq", xv, eye, eye).reshape(GX, 256, 128)
    yi = np.transpose(yf, (0, 2, 1))
    xi = np.transpose(xf, (0, 2, 1))
    return tuple(as_bf16(v) for v in (by_half, depth.T, yf, yi, xf, xi))


def mode_weight(shape):
    lanes = lax.broadcasted_iota(jnp.int32, shape, len(shape) - 1)
    return jnp.where(lax.rem(lanes, MT) == 0, 1.0, 2.0).astype(F32)


def gelu_slope(values):
    normal_cdf = 0.5 * (1.0 + lax.erf(values * (1.0 / math.sqrt(2.0))))
    density = jnp.exp(-0.5 * values * values) * (1.0 / math.sqrt(2.0 * math.pi))
    return normal_cdf + values * density


def mm(a, b):
    return jnp.dot(a, b, preferred_element_type=F32)


class Place:
    def __init__(self):
        self.gx = lax.axis_index("gx")
        self.gy = lax.axis_index("gy")
        self.lo = lax.rem(self.gy, HALF)
        self.hi = lax.div(self.gy, HALF)

    def x_peer(self, d):
        return lax.rem(self.gx + d, GX)

    def y_peer(self, d):
        return lax.rem(self.gy + d, GY)

    def half_peer(self, d):
        return lax.rem(self.lo + d, HALF)

    def greet(self):
        barrier = pltpu.get_barrier_semaphore()
        for d in range(1, GX):
            pl.semaphore_signal(
                barrier, inc=1, device_id={"gx": self.x_peer(d)}, device_id_type=MESH
            )
        for d in range(1, GY):
            pl.semaphore_signal(
                barrier, inc=1, device_id={"gy": self.y_peer(d)}, device_id_type=MESH
            )
        pl.semaphore_wait(barrier, GX + GY - 2)


def remote(src, dst, send, recv, device):
    pltpu.make_async_remote_copy(
        src_ref=src, dst_ref=dst, send_sem=send, recv_sem=recv,
        device_id=device, device_id_type=MESH,
    ).start()


def local(src, dst, sem):
    pltpu.make_async_copy(src, dst, sem).start()


def wait_for(region, sem):
    pltpu.make_async_copy(region, region, sem).wait()


def half_exchange(me, src, dst, send, recv):
    for d in range(1, HALF):
        peer = me.half_peer(d)
        remote(src.at[peer], dst.at[me.lo], send, recv, {"gy": me.hi * HALF + peer})
    local(src.at[me.lo], dst.at[me.lo], recv)


def twin(me, src, dst, send, recv):
    remote(src, dst, send, recv, {"gy": (1 - me.hi) * HALF + me.lo})


def column_exchange(me, src, dst, send, recv):
    for d in range(1, GX):
        peer = me.x_peer(d)
        remote(src.at[peer], dst.at[me.gx], send, recv, {"gx": peer})
    local(src.at[me.gx], dst.at[me.gx], recv)


def column_spread(me, src, dst, send, recv):
    for d in range(1, GX):
        remote(src, dst.at[me.gx], send, recv, {"gx": me.x_peer(d)})
    local(src, dst.at[me.gx], recv)


UNITS = 2 * CHUNKS
SLACK = (2, 2, 2, 2, 2, 2, 2, 2)
FORWARD_SCRATCH = [
    pltpu.VMEM((UNITS, HALF, 64, KZT), BF),
    pltpu.VMEM((UNITS, HALF, 64, KZT), BF),
    pltpu.VMEM((UNITS, 2, HALF, 16, KZT), BF),
    pltpu.VMEM((UNITS, HALF, 16, KZT), BF),
    pltpu.VMEM((UNITS, HALF, 16, KZT), BF),
    pltpu.VMEM((UNITS, HALF, 16, KZT), BF),
    pltpu.VMEM((UNITS, GX, 32, KZT), BF),
    pltpu.VMEM((UNITS, GX, 32, KZT), BF),
    pltpu.SemaphoreType.DMA((4, UNITS)),
    pltpu.SemaphoreType.DMA((4, UNITS)),
]
INVERSE_SCRATCH = [
    pltpu.VMEM((UNITS, 32, KZT), BF),
    pltpu.VMEM((UNITS, GX, 32, KZT), BF),
    pltpu.VMEM((UNITS, HALF, 16, KZT), BF),
    pltpu.VMEM((UNITS, 2, HALF, 16, KZT), BF),
    pltpu.VMEM((UNITS, HALF, 64, KZT), BF),
    pltpu.VMEM((UNITS, HALF, 64, KZT), BF),
    pltpu.SemaphoreType.DMA((4, UNITS)),
    pltpu.SemaphoreType.DMA((4, UNITS)),
]


class Forward:
    def __init__(self, me, depth, yf, xf, sa, ra, half, other, sb, rb, sc, rc, send, recv):
        self.me, self.depth, self.yf, self.xf = me, depth, yf, xf
        self.sa, self.ra, self.sb, self.rb, self.sc, self.rc = sa, ra, sb, rb, sc, rc
        self.half, self.other = half, other
        self.send, self.recv = send, recv

    def sent_a(self, u):
        wait_for(self.sa.at[u, pl.ds(0, HALF - 1)], self.send.at[0, u])

    def sent_b(self, u):
        wait_for(self.other.at[u], self.send.at[1, u])

    def sent_e(self, u):
        wait_for(self.sb.at[u, pl.ds(0, HALF - 1)], self.send.at[2, u])

    def sent_c(self, u):
        wait_for(self.sc.at[u, pl.ds(0, GX - 1)], self.send.at[3, u])

    def put(self, u, table, part, parts, grid):
        count = XL // parts
        modes = mm(grid, table)
        real = modes[:, :128].reshape(count, 2, 2, 1, YL, 128)
        imag = modes[:, 128:].reshape(count, 2, 2, 1, YL, 128)
        both = jnp.concatenate([real, imag], 3)
        both = jnp.concatenate([both[:, 0], both[:, 1]], -1).reshape(count * 32, KZT)
        self.sa[u, pl.ds(part * (count // 2), count // 2)] = both.astype(BF).reshape(
            count // 2, 64, KZT
        )

    def send_a(self, u):
        half_exchange(
            self.me, self.sa.at[u], self.ra.at[u], self.send.at[0, u], self.recv.at[0, u]
        )

    def stage_b(self, u, again):
        wait_for(self.ra.at[u], self.recv.at[0, u])
        if again:
            self.sent_b(u)
        block = self.ra[u].reshape(512, KZT)
        self.half[u] = mm(self.yf[...], block).astype(BF).reshape(2, HALF, 16, KZT)
        twin(
            self.me, self.half.at[u, 1 - self.me.hi], self.other.at[u],
            self.send.at[1, u], self.recv.at[1, u],
        )

    def stage_e(self, u, again):
        wait_for(self.other.at[u], self.recv.at[1, u])
        if again:
            self.sent_e(u)
        mine = self.half[u, pl.ds(self.me.hi, 1)].reshape(HALF, 16, KZT)
        self.sb[u] = (mine.astype(F32) + self.other[u].astype(F32)).astype(BF)
        half_exchange(
            self.me, self.sb.at[u], self.rb.at[u], self.send.at[2, u], self.recv.at[2, u]
        )

    def stage_c(self, u, again):
        wait_for(self.rb.at[u], self.recv.at[2, u])
        if again:
            self.sent_c(u)
        block = self.rb[u].reshape(128, KZT)
        self.sc[u] = mm(self.xf[...], block).astype(BF).reshape(GX, 32, KZT)
        column_exchange(
            self.me, self.sc.at[u], self.rc.at[u], self.send.at[3, u], self.recv.at[3, u]
        )

    def stage_d(self, u, out, weighted):
        wait_for(self.rc.at[u], self.recv.at[3, u])
        total = self.rc[u, 0].astype(F32)
        for source in range(1, GX):
            total = total + self.rc[u, source].astype(F32)
        if weighted:
            total = total * mode_weight(total.shape)
        for kl in range(8):
            for pair in range(2):
                out[u, kl, pair * 4 : pair * 4 + 4, :] = total[
                    kl * 4 : kl * 4 + 4, pair * 128 : pair * 128 + 128
                ]

    def finish(self):
        @pl.loop(0, UNITS)
        def _(u):
            self.sent_a(u)
            self.sent_b(u)
            self.sent_e(u)
            self.sent_c(u)


class Inverse:
    def __init__(self, me, back, yi, xi, spec, rp, sq, rq, sr, rr, send, recv):
        self.me, self.back, self.yi, self.xi, self.spec = me, back, yi, xi, spec
        self.rp, self.sq, self.rq, self.sr, self.rr = rp, sq, rq, sr, rr
        self.send, self.recv = send, recv

    def sent_p(self, u):
        wait_for(self.rp.at[u, pl.ds(0, GX - 1)], self.send.at[0, u])

    def sent_q(self, u):
        wait_for(self.sq.at[u, pl.ds(0, HALF - 1)], self.send.at[1, u])

    def sent_r(self, u):
        wait_for(self.sr.at[u, pl.ds(0, HALF - 1)], self.send.at[3, u])

    def start(self, half, spec, unit, again):
        for c in range(CHUNKS):
            u = half * CHUNKS + c
            for kl in range(8):
                for pair in range(2):
                    unit[kl * 4 : kl * 4 + 4, pair * 128 : pair * 128 + 128] = spec[
                        c, kl, pair * 4 : pair * 4 + 4, :
                    ]
            if again:
                self.sent_p(u)
            self.spec[u] = unit[...].astype(BF)

        @pl.loop(half * CHUNKS, half * CHUNKS + CHUNKS)
        def _(u):
            column_spread(
                self.me, self.spec.at[u], self.rp.at[u], self.send.at[0, u], self.recv.at[0, u]
            )

    def stage_q(self, u, again):
        wait_for(self.rp.at[u], self.recv.at[0, u])
        if again:
            self.sent_q(u)
        block = self.rp[u].reshape(256, KZT)
        self.sq[u] = mm(self.xi[...], block).astype(BF).reshape(HALF, 16, KZT)
        half_exchange(
            self.me, self.sq.at[u], self.rq.at[u, self.me.hi],
            self.send.at[1, u], self.recv.at[1, u],
        )

    def stage_t(self, u):
        mine = self.rq.at[u, self.me.hi]
        wait_for(mine, self.recv.at[1, u])
        twin(self.me, mine, mine, self.send.at[2, u], self.recv.at[2, u])

    def stage_r(self, u, again):
        wait_for(self.rq.at[u, 1 - self.me.hi], self.recv.at[2, u])
        wait_for(self.sq.at[u], self.send.at[2, u])
        if again:
            self.sent_r(u)
        block = self.rq[u].reshape(256, KZT)
        self.sr[u] = mm(self.yi[...], block).astype(BF).reshape(HALF, 64, KZT)
        half_exchange(
            self.me, self.sr.at[u], self.rr.at[u], self.send.at[3, u], self.recv.at[3, u]
        )

    def ready(self, c):
        for half in range(2):
            u = half * CHUNKS + c
            wait_for(self.rr.at[u], self.recv.at[3, u])

    def branch(self, c, part, parts):
        count = XL // parts
        total = None
        for p in range(2):
            halves = []
            for half in range(2):
                block = self.rr[half * CHUNKS + c, pl.ds(part * (count // 2), count // 2)]
                block = block.astype(F32).reshape(count, 2, 2, YL, KZT)[:, :, p]
                block = [block[:, None, :, :, :128], block[:, None, :, :, 128:]]
                halves.append(jnp.concatenate(block, 1))
            lhs = jnp.concatenate(halves, -1).reshape(count * CR, KZT).astype(BF)
            term = mm(lhs, self.back[p * KZT : p * KZT + KZT, :])
            total = term if total is None else total + term
        return total

    def finish(self):
        @pl.loop(0, UNITS)
        def _(u):
            self.sent_p(u)
            self.sent_q(u)
            self.sent_r(u)


def run(schedule):
    steps = max(start + count for start, count, _ in schedule)

    @pl.loop(0, steps)
    def _(t):
        for start, count, stage in schedule:
            @pl.when(jnp.logical_and(t >= start, t < start + count))
            def _(stage=stage, start=start):
                stage(t - start)


TILES = 10
TILE = (TILES, 8, 128)


def swap_parts(tiles):
    even = (lax.rem(lax.broadcasted_iota(jnp.int32, TILE, 1), 2) == 0)
    return jnp.where(even, pltpu.roll(tiles, 7, 1), pltpu.roll(tiles, 1, 1)), even


def coefficient(modes, half, kl, i, part):
    row = pl.ds((i % CC) * 2 + part, 1)
    return jnp.broadcast_to(modes[half * CHUNKS + i // CC, kl, row, :], (8, 128))


def lay_out(modes, half, kl, flat):
    for c in range(CHUNKS):
        for part in range(2):
            flat[pl.ds(c * 16 + half * 2 + part, CC, 4), :] = modes[
                half * CHUNKS + c, kl, pl.ds(part, CC, 2), :
            ]


def mix_modes(modes, half, weight, flat, spec):
    @pl.loop(0, 8)
    def _(kl):
        by_real = jnp.zeros(TILE, F32)
        by_imag = jnp.zeros(TILE, F32)
        for i in range(C):
            block = weight[kl * C + i].astype(F32).reshape(TILE)
            by_real = by_real + block * coefficient(modes, half, kl, i, 0)[None]
            by_imag = by_imag + block * coefficient(modes, half, kl, i, 1)[None]
        turned, even = swap_parts(by_imag)
        mixed = by_real + jnp.where(even, -turned, turned)
        flat[...] = (mixed * mode_weight(TILE)).reshape(80, 128)
        for c in range(CHUNKS):
            for part in range(2):
                spec[c, kl, pl.ds(part, CC, 2), :] = flat[
                    pl.ds(c * 16 + half * 2 + part, CC, 4), :
                ]


def adjoint_modes(scaled, half, weight, flat, sums, spec):
    @pl.loop(0, 8)
    def _(kl):
        lay_out(scaled, half, kl, flat)
        grad = flat[...].reshape(TILE)
        turned, even = swap_parts(grad)
        turned = jnp.where(even, turned, -turned)
        for i in range(C):
            block = weight[kl * C + i].astype(F32).reshape(TILE)
            sums[0, i * 8 : i * 8 + 8] = (block * grad).sum(0)
            sums[1, i * 8 : i * 8 + 8] = (block * turned).sum(0)
        for c in range(CHUNKS):
            for part in range(2):
                total = None
                for row in (0, 1, 4, 5):
                    term = sums[part, pl.ds(c * 32 + half * 2 + row, CC, 8), :]
                    total = term if total is None else total + term
                spec[c, kl, pl.ds(part, CC, 2), :] = total


def gradient_kernel(modes, scaled, field, mixer, bias, out, field_out, mixer_out, bias_out, flat):
    field_out[...] = field[...]
    mixer_out[...] = mixer[...]
    bias_out[...] = bias[...]
    kl = pl.program_id(0)
    for half in range(2):
        lay_out(scaled, half, kl, flat)
    grad = flat[...].reshape(TILE)
    turned, even = swap_parts(grad)
    turned = jnp.where(even, turned, -turned)
    first = lax.rem(lax.broadcasted_iota(jnp.int32, (8, 128), 0), 4) < 2
    for i in range(C):
        real, imag = (
            jnp.where(first, coefficient(modes, 0, kl, i, p), coefficient(modes, 1, kl, i, p))
            for p in range(2)
        )
        out[i] = (grad * real[None] + turned * imag[None]).reshape(80, 128)


def channel_rows():
    rows = lax.broadcasted_iota(jnp.int32, (ROWS, C), 0)
    return lax.div(rows, YL) == lax.broadcasted_iota(jnp.int32, (ROWS, C), 1)


def same_place():
    rows = lax.broadcasted_iota(jnp.int32, (ROWS, ROWS), 0)
    columns = lax.broadcasted_iota(jnp.int32, (ROWS, ROWS), 1)
    return lax.rem(rows, YL) == lax.rem(columns, YL)


def spread_mixer(mixer, axis):
    spread = jnp.where(channel_rows(), 1.0, 0.0).astype(BF)
    half = lax.dot_general(
        spread, mixer, (((1,), (1 - axis,)), ((), ())), preferred_element_type=F32
    ).astype(BF)
    full = lax.dot_general(
        half, spread, (((1,), (1,)), ((), ())), preferred_element_type=F32
    )
    return jnp.where(same_place(), full, 0.0).astype(BF)


FORWARD_TABLES = [
    pltpu.VMEM((2, NZT, KZT), BF),
    pltpu.VMEM((256, 512), BF),
    pltpu.VMEM((256, 128), BF),
    pltpu.SemaphoreType.DMA((3,)),
]
INVERSE_TABLES = [
    pltpu.VMEM((2 * KZT, NZT), BF),
    pltpu.VMEM((512, 256), BF),
    pltpu.VMEM((128, 256), BF),
    pltpu.SemaphoreType.DMA((3,)),
]


def fetch_tables(me, depth_hbm, y_hbm, x_hbm, depth, y, x, sem):
    pairs = ((depth_hbm, depth), (y_hbm.at[me.hi], y), (x_hbm.at[me.gx], x))
    for n, (src, dst) in enumerate(pairs):
        local(src, dst, sem.at[n])

    def ready():
        for n, (_, dst) in enumerate(pairs):
            wait_for(dst, sem.at[n])

    return ready


def whole_kernel(
    x_hbm, cot_hbm, weight_hbm, mixer, bias, depth_hbm, yf_hbm, xf_hbm, back_hbm, yi_hbm, xi_hbm,
    out_hbm, modes, scaled, mixer_out, bias_out,
    gbuf, cbuf, point, weight, flat, sums, spec, unit, mixed, one, col, two, row,
    gsem, csem, wsem, small, *scratch
):
    me = Place()
    n = len(FORWARD_TABLES)
    depth, yf, xf, tsem, back, yi, xi, isem = scratch[: 2 * n]
    scratch = scratch[2 * n :]

    def chunk_of(ref, c):
        return ref.at[:, pl.ds(c * CR, CR), :]

    local(chunk_of(x_hbm, 0), gbuf.at[0], gsem.at[0])
    forward_ready = fetch_tables(me, depth_hbm, yf_hbm, xf_hbm, depth, yf, xf, tsem)

    @pl.loop(1, CHUNKS)
    def _(c):
        local(chunk_of(x_hbm, c), gbuf.at[c], gsem.at[c])

    local(weight_hbm, weight, wsem)
    inverse_ready = fetch_tables(me, back_hbm, yi_hbm, xi_hbm, back, yi, xi, isem)

    @pl.loop(0, CHUNKS)
    def _(c):
        local(chunk_of(cot_hbm, c), cbuf.at[c], csem.at[c])

    me.greet()
    n = len(INVERSE_SCRATCH)
    inv = Inverse(me, back, yi, xi, *scratch[:n])
    fwd = Forward(me, depth, yf, xf, *scratch[n:])
    flat[...] = jnp.zeros_like(flat)
    mixed[...] = jnp.zeros_like(mixed)
    forward_ready()

    def first_a(u):
        c = lax.rem(u, CHUNKS)

        @pl.when(u < CHUNKS)
        def _():
            wait_for(gbuf.at[c], gsem.at[c])

        table = depth[lax.div(u, CHUNKS)]
        for part in range(2):
            fwd.put(u, table, part, 2, gbuf[c, part * 8 : part * 8 + 8].reshape(8 * CR, NZT))
        fwd.send_a(u)

    def spectrum(half):
        if half == 0:
            wait_for(weight, wsem)
            inverse_ready()
        mix_modes(modes, half, weight, flat, spec)
        inv.start(half, spec, unit, False)

    def back_spectrum(half):
        adjoint_modes(scaled, half, weight, flat, sums, spec)
        inv.start(half, spec, unit, True)

    def pointwise(n):
        spread = spread_mixer(mixer[...], 0)
        shift = jnp.where(channel_rows(), bias[...], 0.0).sum(1, keepdims=True)
        for x in (2 * n, 2 * n + 1):
            point[x] = mm(spread, gbuf[:, x].reshape(ROWS, NZT)) + shift

    def slope(c):
        inv.ready(c)
        wait_for(cbuf.at[c], csem.at[c])
        fwd.sent_a(c)
        fwd.sent_a(CHUNKS + c)

        @pl.loop(0, 2)
        def _(part):
            rows = pl.ds(part * 8, 8)
            pre = inv.branch(c, part, 2)
            pre = pre + point[rows, pl.ds(c * CR, CR), :].reshape(8 * CR, NZT)
            cot = cbuf[c, rows].reshape(8 * CR, NZT).astype(F32)
            grad = (cot * gelu_slope(pre)).astype(BF)
            gbuf[c, rows] = grad.reshape(8, CR, NZT)
            for half in range(2):
                fwd.put(half * CHUNKS + c, depth[half], part, 2, grad)

        local(chunk_of(x_hbm, c), cbuf.at[c], csem.at[c])

    def pointwise_back(n):
        @pl.when(n == 0)
        def _():
            @pl.loop(0, CHUNKS)
            def _(c):
                wait_for(cbuf.at[c], csem.at[c])

        spread = spread_mixer(mixer[...], 1)
        contract = (((1,), (1,)), ((), ()))
        for x in (2 * n, 2 * n + 1):
            grad = gbuf[:, x].reshape(ROWS, NZT)
            point[x] = mm(spread, grad)
            mixed[:ROWS, :] += lax.dot_general(
                cbuf[:, x].reshape(ROWS, NZT), grad, contract, preferred_element_type=F32
            )
            mixed[ROWS:, :] += lax.dot_general(
                jnp.ones((8, NZT), BF), grad, contract, preferred_element_type=F32
            )

    def across_columns(_):
        kept = jnp.where(same_place(), mixed[:ROWS, :], 0.0).reshape(C, YL, ROWS).sum(1)
        stacked = jnp.concatenate([kept, mixed[ROWS : ROWS + 4, :]], 0)
        fold = lax.div(lax.broadcasted_iota(jnp.int32, (ROWS, 128), 0), YL)
        fold = fold == lax.broadcasted_iota(jnp.int32, (ROWS, 128), 1)
        one[...] = lax.dot_general(
            stacked, jnp.where(fold, 1.0, 0.0), (((1,), (0,)), ((), ())),
            precision=lax.Precision.HIGHEST, preferred_element_type=F32,
        )
        for d in range(1, GX):
            remote(one, col.at[me.gx], small.at[0], small.at[1], {"gx": me.x_peer(d)})
        local(one, col.at[me.gx], small.at[1])

    def across_rows(_):
        wait_for(col, small.at[1])
        total = col[0]
        for source in range(1, GX):
            total = total + col[source]
        two[...] = total
        for d in range(1, GY):
            remote(two, row.at[me.gy], small.at[2], small.at[3], {"gy": me.y_peer(d)})
        local(two, row.at[me.gy], small.at[3])

    def result(c):
        inv.ready(c)

        @pl.loop(0, 2)
        def _(part):
            rows = pl.ds(part * 8, 8)
            total = inv.branch(c, part, 2)
            total = total + point[rows, pl.ds(c * CR, CR), :].reshape(8 * CR, NZT)
            gbuf[c, rows] = total.astype(BF).reshape(8, CR, NZT)

        local(gbuf.at[c], chunk_of(out_hbm, c), gsem.at[c])

    send_b, send_e, send_c, send_d, send_q, send_t, send_r, send_s = SLACK
    at_b = send_b
    at_e = at_b + send_e
    at_c = at_e + send_c
    at_d = at_c + send_d
    at_p = at_d + CHUNKS - 1
    at_q = at_p + send_q
    at_t = at_q + send_t
    at_r = at_t + send_r
    at_s = at_r + CHUNKS + send_s
    run([
        (0, UNITS, first_a),
        (at_b, UNITS, lambda u: fwd.stage_b(u, False)),
        (at_e, UNITS, lambda u: fwd.stage_e(u, False)),
        (at_c, UNITS, lambda u: fwd.stage_c(u, False)),
        (at_d, UNITS, lambda u: fwd.stage_d(u, modes, False)),
        (5, 8, pointwise),
        (at_p, 1, lambda _: spectrum(0)),
        (at_p + CHUNKS, 1, lambda _: spectrum(1)),
        (at_q, UNITS, lambda u: inv.stage_q(u, False)),
        (at_t, UNITS, inv.stage_t),
        (at_r, UNITS, lambda u: inv.stage_r(u, False)),
        (at_s, CHUNKS, slope),
        (at_s, UNITS, fwd.send_a),
        (at_s + at_b, UNITS, lambda u: fwd.stage_b(u, True)),
        (at_s + at_e, UNITS, lambda u: fwd.stage_e(u, True)),
        (at_s + at_c, UNITS, lambda u: fwd.stage_c(u, True)),
        (at_s + at_d, UNITS, lambda u: fwd.stage_d(u, scaled, True)),
        (at_s + 5, 8, pointwise_back),
        (at_s + at_p, 1, lambda _: back_spectrum(0)),
        (at_s + at_p + CHUNKS, 1, lambda _: back_spectrum(1)),
        (at_s + at_q, UNITS, lambda u: inv.stage_q(u, True)),
        (at_s + at_t, UNITS, inv.stage_t),
        (at_s + at_r, UNITS, lambda u: inv.stage_r(u, True)),
        (at_s + 13, 1, across_columns),
        (at_s + 15, 1, across_rows),
        (at_s + at_s, CHUNKS, result),
    ])

    wait_for(row, small.at[3])
    total = row[0]
    for source in range(1, GY):
        total = total + row[source]
    total = total * (1.0 / math.sqrt(NX * NY * NZT))
    mixer_out[...] = total[:C, :C]
    bias_out[...] = total[C : C + 1, :C]
    wait_for(col.at[pl.ds(0, GX - 1)], small.at[0])
    wait_for(row.at[pl.ds(0, GY - 1)], small.at[2])

    @pl.loop(0, CHUNKS)
    def _(c):
        wait_for(gbuf.at[c], gsem.at[c])

    inv.finish()
    fwd.finish()


ANY = pl.BlockSpec(memory_space=pl.ANY)
VM = pl.BlockSpec(memory_space=pltpu.VMEM)


def params(number):
    return pltpu.CompilerParams(
        collective_id=number, has_side_effects=True, vmem_limit_bytes=60 * 2**20
    )


def body(layer_input, cotangent, spectral_weight, mixer_weight, bias_vector):
    depth, back, yf, yi, xf, xi = (jnp.asarray(v) for v in tables())
    grid = jnp.swapaxes(layer_input, 1, 2).reshape(XL, ROWS, NZT)
    cot = jnp.swapaxes(cotangent, 1, 2).reshape(XL, ROWS, NZT)
    weight = spectral_weight.reshape(8 * C, C, 2, 2, 128)
    weight = jnp.swapaxes(weight, 2, 3).reshape(8 * C, 4 * C, 128)
    modes_shape = jax.ShapeDtypeStruct((UNITS, 8, 8, 128), F32)
    chunked = pltpu.VMEM((CHUNKS, XL, CR, NZT), BF)
    chunk_sems = pltpu.SemaphoreType.DMA((CHUNKS,))
    flat = pltpu.VMEM((4 * C, 128), F32)

    input_grad, modes, scaled, mixer_grad, bias_grad = pl.pallas_call(
        whole_kernel,
        out_shape=[
            jax.ShapeDtypeStruct((XL, ROWS, NZT), BF),
            modes_shape,
            modes_shape,
            jax.ShapeDtypeStruct((C, C), F32),
            jax.ShapeDtypeStruct((1, C), F32),
        ],
        in_specs=[ANY, ANY, ANY, VM, VM] + [ANY] * 6,
        out_specs=[ANY, VM, VM, VM, VM],
        scratch_shapes=[
            chunked,
            chunked,
            pltpu.VMEM((XL, ROWS, NZT), F32),
            pltpu.VMEM((8 * C, 4 * C, 128), BF),
            flat,
            pltpu.VMEM((2, 8 * C, 128), F32),
            pltpu.VMEM((CHUNKS, 8, 8, 128), F32),
            pltpu.VMEM((32, KZT), F32),
            pltpu.VMEM((ROWS + 8, ROWS), F32),
            pltpu.VMEM((24, 128), F32),
            pltpu.VMEM((GX, 24, 128), F32),
            pltpu.VMEM((24, 128), F32),
            pltpu.VMEM((GY, 24, 128), F32),
            chunk_sems,
            chunk_sems,
            pltpu.SemaphoreType.DMA,
            pltpu.SemaphoreType.DMA((4,)),
        ]
        + FORWARD_TABLES
        + INVERSE_TABLES
        + INVERSE_SCRATCH
        + FORWARD_SCRATCH,
        compiler_params=params(1),
        name="whole",
    )(grid, cot, weight, mixer_weight, bias_vector.reshape(1, C), depth, yf, xf, back, yi, xi)

    field_spec = pl.BlockSpec((XL // 8, ROWS, NZT), lambda kl: (kl, 0, 0))
    modes_spec = pl.BlockSpec((UNITS, 8, 8, 128), lambda kl: (0, 0, 0, 0))
    spectral_grad, input_grad, mixer_grad, bias_grad = pl.pallas_call(
        gradient_kernel,
        out_shape=[
            jax.ShapeDtypeStruct((8 * C, 4 * C, 128), F32),
            jax.ShapeDtypeStruct((XL, ROWS, NZT), BF),
            jax.ShapeDtypeStruct((C, C), F32),
            jax.ShapeDtypeStruct((1, C), F32),
        ],
        grid=(8,),
        in_specs=[modes_spec, modes_spec, field_spec, VM, VM],
        out_specs=[pl.BlockSpec((C, 4 * C, 128), lambda kl: (kl, 0, 0)), field_spec, VM, VM],
        scratch_shapes=[flat],
        name="gradient",
    )(modes, scaled, input_grad, mixer_grad, bias_grad)
    spectral_grad = jnp.swapaxes(spectral_grad.reshape(8 * C, C, 2, 2, 128), 2, 3)
    spectral_grad = spectral_grad.reshape(4, 2, C, C, 2, KZT)
    input_grad = jnp.swapaxes(input_grad.reshape(XL, C, YL, NZT), 1, 2)
    return (input_grad, spectral_grad, mixer_grad, bias_grad.reshape(C))


def solution(mesh):
    return jax.shard_map(
        body,
        mesh=mesh,
        in_specs=(
            P("gx", "gy", None, None),
            P("gx", "gy", None, None),
            P("gx", "gy", None, None, None, None),
            P(),
            P(),
        ),
        out_specs=(P("gx", "gy", None, None), P("gx", "gy", None, None, None, None), P(), P()),
        check_vma=False,
    )
```

time: 244 us -> 215 us (0.88)
  Pallas kernels: 236 us -> 214 us
  local copies, waits for them, and re-layouts: 6.77 us -> 0 us
    pallas_call x4 -> x2, Pallas kernels: 236 us -> 214 us  [the longest x1 205 us: body(): pl.pallas_call(whole_kernel, out_shape=[jax.ShapeDtypeStruct((XL, ROWS, N...]
    unnamed x7 -> x0, local copies, waits for them, and re-layouts: 6.77 us -> none
where the time goes in v3:
time: 215 us
  Pallas kernels  214 us (100%)
    pallas_call x1, Pallas kernels, body(): pl.pallas_call(whole_kernel, out_shape=[jax.ShapeDtypeStruct((XL, ROWS, N...  205 us
    pallas_call x1, Pallas kernels, body(): pl.pallas_call(gradient_kernel, out_shape=[jax.ShapeDtypeStruct((8 * C, 4...  8.46 us

profile of v3, /device:TPU:1, one launch (start us, length us, event | category | flops | bytes accessed | tf_op | source)
XLA Modules:
  0.0 214.5 jit_solution(10732792446147563898)
XLA Ops:
  0.6 205.4 %whole.1 = (bf16[16,160,1024]{2,1,0:T(8,128)(2,1)}, f32[10,8,8,128]{3,2,1,0:T(8,128)}, f32[10,8,8,128]{3,2,1,0:T(8,128)}, f32[20,20]{1,0:T(8,128)}, f32[1,20]{1,0:T(1,128)}) custom-call(bf16[16,160,1024]{2,1,0:T(8,128)(2,1)} %bitcast.21, bf16[16,160,1024]{2,1,0:T(8,128)(2,1)} %bitcast.22, bf16[160,80,128]{2,1,0:T(8,128)(2,1)} %bitcast.23, ...), custom_call_target="tpu_custom_call" | custom-call | tf_op jit(solution)/shard_map/whole/pallas_call | solution.py:731
  206.1 8.5 %gradient.1 = (f32[160,80,128]{2,1,0:T(8,128)}, bf16[16,160,1024]{2,1,0:T(8,128)(2,1)}, f32[20,20]{1,0:T(8,128)}, f32[1,20]{1,0:T(1,128)}) custom-call(f32[10,8,8,128]{3,2,1,0:T(8,128)} %get-tuple-element.13.modes, f32[10,8,8,128]{3,2,1,0:T(8,128)} %get-tuple-element.14.scaled, bf16[16,160,1024]{2,1,0:T(8,128)(2,1)} %get-tuple-element.15.field, ...), custom_call_target="tpu_custom_call" | custom-call | tf_op jit(solution)/shard_map/gradient/pallas_call | solution.py:771

commit v4 on v3

--- a/solution.py
+++ b/solution.py
@@ -661,29 +661,29 @@
     at_r = at_t + send_r
     at_s = at_r + CHUNKS + send_s
     run([
+        (at_e, UNITS, lambda u: fwd.stage_e(u, False)),
+        (at_s + at_e, UNITS, lambda u: fwd.stage_e(u, True)),
+        (at_c, UNITS, lambda u: fwd.stage_c(u, False)),
+        (at_s + at_c, UNITS, lambda u: fwd.stage_c(u, True)),
+        (at_d, UNITS, lambda u: fwd.stage_d(u, modes, False)),
+        (at_s + at_d, UNITS, lambda u: fwd.stage_d(u, scaled, True)),
+        (at_q, UNITS, lambda u: inv.stage_q(u, False)),
+        (at_s + at_q, UNITS, lambda u: inv.stage_q(u, True)),
+        (at_t, UNITS, inv.stage_t),
+        (at_s + at_t, UNITS, inv.stage_t),
+        (at_b, UNITS, lambda u: fwd.stage_b(u, False)),
+        (at_s + at_b, UNITS, lambda u: fwd.stage_b(u, True)),
+        (at_r, UNITS, lambda u: inv.stage_r(u, False)),
+        (at_s + at_r, UNITS, lambda u: inv.stage_r(u, True)),
         (0, UNITS, first_a),
-        (at_b, UNITS, lambda u: fwd.stage_b(u, False)),
-        (at_e, UNITS, lambda u: fwd.stage_e(u, False)),
-        (at_c, UNITS, lambda u: fwd.stage_c(u, False)),
-        (at_d, UNITS, lambda u: fwd.stage_d(u, modes, False)),
+        (at_s, CHUNKS, slope),
+        (at_s, UNITS, fwd.send_a),
         (5, 8, pointwise),
         (at_p, 1, lambda _: spectrum(0)),
         (at_p + CHUNKS, 1, lambda _: spectrum(1)),
-        (at_q, UNITS, lambda u: inv.stage_q(u, False)),
-        (at_t, UNITS, inv.stage_t),
-        (at_r, UNITS, lambda u: inv.stage_r(u, False)),
-        (at_s, CHUNKS, slope),
-        (at_s, UNITS, fwd.send_a),
-        (at_s + at_b, UNITS, lambda u: fwd.stage_b(u, True)),
-        (at_s + at_e, UNITS, lambda u: fwd.stage_e(u, True)),
-        (at_s + at_c, UNITS, lambda u: fwd.stage_c(u, True)),
-        (at_s + at_d, UNITS, lambda u: fwd.stage_d(u, scaled, True)),
-        (at_s + 5, 8, pointwise_back),
         (at_s + at_p, 1, lambda _: back_spectrum(0)),
         (at_s + at_p + CHUNKS, 1, lambda _: back_spectrum(1)),
-        (at_s + at_q, UNITS, lambda u: inv.stage_q(u, True)),
-        (at_s + at_t, UNITS, inv.stage_t),
-        (at_s + at_r, UNITS, lambda u: inv.stage_r(u, True)),
+        (at_s + 5, 8, pointwise_back),
         (at_s + 13, 1, across_columns),
         (at_s + 15, 1, across_rows),
         (at_s + at_s, CHUNKS, result),

time: 215 us -> 213 us (level)
    pallas_call x1, Pallas kernels: 205 us -> 203 us  [body(): pl.pallas_call(whole_kernel, out_shape=[jax.ShapeDtypeStruct((XL, ROWS, N...]
where the time goes in v4:
time: 213 us; the launch traced here: 212 us
  Pallas kernels  212 us (100%)
    pallas_call x1, Pallas kernels, body(): pl.pallas_call(whole_kernel, out_shape=[jax.ShapeDtypeStruct((XL, ROWS, N...  203 us
    pallas_call x1, Pallas kernels, body(): pl.pallas_call(gradient_kernel, out_shape=[jax.ShapeDtypeStruct((8 * C, 4...  8.46 us

profile of v4, /device:TPU:1, one launch (start us, length us, event | category | flops | bytes accessed | tf_op | source)
XLA Modules:
  0.0 212.2 jit_solution(10507591781196902639)
XLA Ops:
  0.6 203.1 %whole.1 = (bf16[16,160,1024]{2,1,0:T(8,128)(2,1)}, f32[10,8,8,128]{3,2,1,0:T(8,128)}, f32[10,8,8,128]{3,2,1,0:T(8,128)}, f32[20,20]{1,0:T(8,128)}, f32[1,20]{1,0:T(1,128)}) custom-call(bf16[16,160,1024]{2,1,0:T(8,128)(2,1)} %bitcast.21, bf16[16,160,1024]{2,1,0:T(8,128)(2,1)} %bitcast.22, bf16[160,80,128]{2,1,0:T(8,128)(2,1)} %bitcast.23, ...), custom_call_target="tpu_custom_call" | custom-call | tf_op jit(solution)/shard_map/whole/pallas_call | solution.py:731
  203.7 8.5 %gradient.1 = (f32[160,80,128]{2,1,0:T(8,128)}, bf16[16,160,1024]{2,1,0:T(8,128)(2,1)}, f32[20,20]{1,0:T(8,128)}, f32[1,20]{1,0:T(1,128)}) custom-call(f32[10,8,8,128]{3,2,1,0:T(8,128)} %get-tuple-element.13.modes, f32[10,8,8,128]{3,2,1,0:T(8,128)} %get-tuple-element.14.scaled, bf16[16,160,1024]{2,1,0:T(8,128)(2,1)} %get-tuple-element.15.field, ...), custom_call_target="tpu_custom_call" | custom-call | tf_op jit(solution)/shard_map/gradient/pallas_call | solution.py:771

commit v5 on v4

--- a/solution.py
+++ b/solution.py
@@ -172,7 +172,7 @@
 
 
 UNITS = 2 * CHUNKS
-SLACK = (2, 2, 2, 2, 2, 2, 2, 2)
+SLACK = (2, 2, 3, 3, 2, 3, 3, 2)
 FORWARD_SCRATCH = [
     pltpu.VMEM((UNITS, HALF, 64, KZT), BF),
     pltpu.VMEM((UNITS, HALF, 64, KZT), BF),

time: 213 us -> 222 us (1.042)
  Pallas kernels: 212 us -> 221 us
    pallas_call x1, Pallas kernels: 203 us -> 212 us  [body(): pl.pallas_call(whole_kernel, out_shape=[jax.ShapeDtypeStruct((XL, ROWS, N...]
where the time goes in v5:
time: 222 us
  Pallas kernels  221 us (100%)
    pallas_call x1, Pallas kernels, body(): pl.pallas_call(whole_kernel, out_shape=[jax.ShapeDtypeStruct((XL, ROWS, N...  212 us
    pallas_call x1, Pallas kernels, body(): pl.pallas_call(gradient_kernel, out_shape=[jax.ShapeDtypeStruct((8 * C, 4...  8.46 us

profile of v5, /device:TPU:1, one launch (start us, length us, event | category | flops | bytes accessed | tf_op | source)
XLA Modules:
  0.0 221.6 jit_solution(16812378810950493383)
XLA Ops:
  0.6 212.5 %whole.1 = (bf16[16,160,1024]{2,1,0:T(8,128)(2,1)}, f32[10,8,8,128]{3,2,1,0:T(8,128)}, f32[10,8,8,128]{3,2,1,0:T(8,128)}, f32[20,20]{1,0:T(8,128)}, f32[1,20]{1,0:T(1,128)}) custom-call(bf16[16,160,1024]{2,1,0:T(8,128)(2,1)} %bitcast.21, bf16[16,160,1024]{2,1,0:T(8,128)(2,1)} %bitcast.22, bf16[160,80,128]{2,1,0:T(8,128)(2,1)} %bitcast.23, ...), custom_call_target="tpu_custom_call" | custom-call | tf_op jit(solution)/shard_map/whole/pallas_call | solution.py:731
  213.1 8.5 %gradient.1 = (f32[160,80,128]{2,1,0:T(8,128)}, bf16[16,160,1024]{2,1,0:T(8,128)(2,1)}, f32[20,20]{1,0:T(8,128)}, f32[1,20]{1,0:T(1,128)}) custom-call(f32[10,8,8,128]{3,2,1,0:T(8,128)} %get-tuple-element.13.modes, f32[10,8,8,128]{3,2,1,0:T(8,128)} %get-tuple-element.14.scaled, bf16[16,160,1024]{2,1,0:T(8,128)(2,1)} %get-tuple-element.15.field, ...), custom_call_target="tpu_custom_call" | custom-call | tf_op jit(solution)/shard_map/gradient/pallas_call | solution.py:771
